TPU v7x, 32 devices: a whole 2x2x4 slice. The times are simulated.
32 devices in a mesh: dp: 8 (over z, x), mp: 4 (over y, core).
Axes of the slice: x: 2, y: 2, z: 4, core: 2. Of those that a mesh axis runs over, the one named last changes fastest.
Arguments:
- tokens: bfloat16 [16384, 768], P('dp'), may hold values from -6 to 6
- lengths: int32 [8, 3], P('dp'), may hold values from 1 to 1792, 2048 in all within a row
- norm_gain: bfloat16 [2, 2, 768], P(None, None, 'dp'), may hold values from 0.099609375 to 1.8984375
- w_value: bfloat16 [2, 768, 768], P(None, 'dp', 'mp'), may hold values from -0.21875 to 0.21875
- w_out: bfloat16 [2, 768, 768], P(None, 'mp', 'dp'), may hold values from -0.875 to 0.875
- w_up: bfloat16 [2, 768, 3072], P(None, 'dp', 'mp'), may hold values from -0.21875 to 0.21875
- w_down: bfloat16 [2, 3072, 768], P(None, 'mp', 'dp'), may hold values from -0.109375 to 0.109375
- synth_first: bfloat16 [768, 768], P('dp', 'mp'), may hold values from -0.21875 to 0.21875
- synth_second: bfloat16 [12, 64, 2048], P('mp', None, 'dp'), may hold values from -4 to 4
- random_table: bfloat16 [12, 2048, 2048], P('mp', 'dp'), may hold values from -9 to 9
- cotangent: bfloat16 [16384, 768], P('dp'), may hold values from -6 to 6
Outputs:
- layer_output: bfloat16 [16384, 768], P('dp')
- input_grad: bfloat16 [16384, 768], P('dp')
- gain_grad: float32 [2, 2, 768], P(None, None, 'dp')
- value_grad: float32 [2, 768, 768], P(None, 'dp', 'mp')
- out_grad: float32 [2, 768, 768], P(None, 'mp', 'dp')
- up_grad: float32 [2, 768, 3072], P(None, 'dp', 'mp')
- down_grad: float32 [2, 3072, 768], P(None, 'mp', 'dp')
- first_grad: float32 [768, 768], P('dp', 'mp')
- second_grad: float32 [12, 64, 2048], P('mp', None, 'dp')
- random_grad: float32 [12, 2048, 2048], P('mp', 'dp')
Inputs may be any that keep to these rules, and one draw needn't show every extreme that they name: Each row lists the lengths of the 3 items of one slot; a row sums to 2048 and its longest item is 1792.
All inputs are finite; a program needn't handle non-finite values.
Results may differ from a plain program's by a relative error of at most 0.023.
Values may be sent and summed in bfloat16 or wider, within the bound.
A program may use at most 448 MiB of HBM per device.

v0:
```python
from functools import partial

import jax
import jax.numpy as jnp
from jax import lax
from jax.experimental import pallas as pl
from jax.experimental.pallas import tpu as pltpu
from jax.sharding import PartitionSpec as P

F32, BF16 = jnp.float32, jnp.bfloat16
HD = 64
MOST = 1792
TILE = 256
VMEM = 58 * 1024 * 1024


MESH = pl.DeviceIdType.MESH
ANY = pl.BlockSpec(memory_space=pl.ANY)
INTO = pl.BlockSpec(memory_space=pltpu.VMEM)
SCALAR = pl.BlockSpec(memory_space=pltpu.SMEM)
DMA = pltpu.SemaphoreType.DMA


def remote(source, target, send, recv, axis, index):
    return pltpu.make_async_remote_copy(
        src_ref=source, dst_ref=target, send_sem=send, recv_sem=recv, device_id={axis: index}, device_id_type=MESH
    )


def greet(groups):
    barrier = pltpu.get_barrier_semaphore()
    for axis, size in groups:
        me = lax.axis_index(axis)
        for step in range(1, size):
            pl.semaphore_signal(
                barrier, inc=1, device_id={axis: lax.rem(me + step, size)}, device_id_type=MESH
            )
    pl.semaphore_wait(barrier, sum(size - 1 for _, size in groups))


def greet_all(n, n_mp):
    barrier = pltpu.get_barrier_semaphore()
    me = lax.axis_index("dp") * n_mp + lax.axis_index("mp")

    @pl.loop(1, n * n_mp)
    def _(step):
        there = lax.rem(me + step, n * n_mp)
        where = {"dp": there // n_mp, "mp": lax.rem(there, n_mp)}
        pl.semaphore_signal(barrier, inc=1, device_id=where, device_id_type=MESH)

    pl.semaphore_wait(barrier, n * n_mp - 1)


def remote_to(source, target, send, recv, place, rank):
    return pltpu.make_async_remote_copy(
        src_ref=source,
        dst_ref=target,
        send_sem=send,
        recv_sem=recv,
        device_id={"dp": place, "mp": rank},
        device_id_type=MESH,
    )


def comm_params(number):
    return pltpu.CompilerParams(collective_id=number, has_side_effects=True, vmem_limit_bytes=VMEM)


class Line:
    def __init__(self, size):
        self.size, self.length = size, size // 2
        self.place = lax.axis_index("dp")
        self.at, self.side = self.place // 2, lax.rem(self.place, 2)
        self.partner = self.at * 2 + 1 - self.side
        self.right, self.left = self.place + 2, self.place - 2
        self.has_right, self.has_left = self.at + 1 < self.length, self.at > 0


class Gather:
    def __init__(self, line, pieces, use, even=False):
        self.line, self.pieces, self.use = line, pieces, use
        self.even = even and line.length == 4

    def block(self, slots, s, half=None):
        if half is None:
            return slots.at[s]
        rows = slots.shape[1] // 2
        return slots.at[s, pl.ds(half * rows, rows)]

    def push(self, piece, s, to, send, fresh=False, half=None, recv=None):
        own, slots = piece[:2]
        target = self.block(slots, s, half)
        remote(own if fresh else target, target, send, piece[4].at[s] if recv is None else recv, "dp", to).start()

    def arrived(self, piece, s, half=None, recv=None):
        target = self.block(piece[1], s, half)
        recv = piece[4].at[s] if recv is None else recv
        remote(target, target, piece[2].at[0], recv, "dp", self.line.partner).wait_recv()

    def sent(self, which, half=None):
        for piece in self.pieces:
            target = self.block(piece[1], 0, half)
            remote(target, target, which(piece), piece[4].at[0], "dp", self.line.partner).wait_send()

    def start(self, piece):
        line = self.line

        @pl.when(line.has_right)
        def _():
            self.push(piece, line.place, line.right, piece[3].at[0, line.at], fresh=True)

        @pl.when(line.has_left)
        def _():
            self.push(piece, line.place, line.left, piece[3].at[1, line.at], fresh=True)

        self.push(piece, line.place, line.partner, piece[2].at[line.at], fresh=True)

    def spared(self, a):
        at = self.line.at
        half = jnp.logical_or(jnp.logical_and(at == 0, a == 3), jnp.logical_and(at == 3, a == 0))
        none = jnp.logical_or(jnp.logical_and(at == 1, a == 0), jnp.logical_and(at == 2, a == 3))
        return jnp.logical_not(jnp.logical_or(half, none)), half

    def arrive(self, a, way):
        line = self.line
        s = a * 2 + line.side
        on, to = ((line.has_right, line.right), (line.has_left, line.left))[way]
        for piece in self.pieces:
            self.arrived(piece, s)

            @pl.when(on)
            def _():
                self.push(piece, s, to, piece[3].at[way, a])

            if self.even:
                whole, half = self.spared(a)

                @pl.when(whole)
                def _():
                    self.push(piece, s, line.partner, piece[2].at[a])

                @pl.when(half)
                def _():
                    self.push(piece, s, line.partner, piece[2].at[a], half=0)
            else:
                self.push(piece, s, line.partner, piece[2].at[a])
            piece[6](s)

    def crossed(self, a):
        line = self.line
        at = line.at
        s = a * 2 + 1 - line.side
        for piece in self.pieces:
            if self.even:
                _, half = self.spared(a)
                send, recv = piece[5].at[0], piece[5].at[1]

                @pl.when(half)
                def _():
                    self.arrived(piece, s, half=0)
                    self.arrived(piece, s, half=1, recv=recv)

                @pl.when(jnp.logical_not(half))
                def _():
                    self.arrived(piece, s)

                @pl.when(jnp.logical_and(at == 0, a == 0))
                def _():
                    self.push(piece, s, line.right, send)

                @pl.when(jnp.logical_and(at == 3, a == 3))
                def _():
                    self.push(piece, s, line.left, send)

                @pl.when(jnp.logical_and(at == 1, a == 3))
                def _():
                    self.push(piece, s, line.left, send, half=1, recv=recv)

                @pl.when(jnp.logical_and(at == 2, a == 0))
                def _():
                    self.push(piece, s, line.right, send, half=1, recv=recv)
            else:
                self.arrived(piece, s)
            piece[6](s)
        self.use(s)

    def step(self, k):
        line = self.line
        low, high = line.at - k, line.at + k

        @pl.when(low >= 0)
        def _():
            self.arrive(low, 0)

        @pl.when(high < line.length)
        def _():
            self.arrive(high, 1)

        @pl.when(low >= 0)
        def _():
            self.use(low * 2 + line.side)

        @pl.when(high < line.length)
        def _():
            self.use(high * 2 + line.side)

        @pl.when(low + 1 >= 0)
        def _():
            self.crossed(low + 1)

        @pl.when(jnp.logical_and(k > 1, high - 1 < line.length))
        def _():
            self.crossed(high - 1)

    def end(self):
        line = self.line

        @pl.loop(0, line.length)
        def _(a):
            if self.even:
                whole, half = self.spared(a)

                @pl.when(whole)
                def _():
                    self.sent(lambda piece: piece[2].at[a])

                @pl.when(half)
                def _():
                    self.sent(lambda piece: piece[2].at[a], half=0)
            else:
                self.sent(lambda piece: piece[2].at[a])

            @pl.when(jnp.logical_and(line.has_right, a <= line.at))
            def _():
                self.sent(lambda piece: piece[3].at[0, a])

            @pl.when(jnp.logical_and(line.has_left, a >= line.at))
            def _():
                self.sent(lambda piece: piece[3].at[1, a])

        if self.even:
            outer = jnp.logical_or(line.at == 0, line.at == 3)

            @pl.when(outer)
            def _():
                self.sent(lambda piece: piece[5].at[0])

            @pl.when(jnp.logical_not(outer))
            def _():
                self.sent(lambda piece: piece[5].at[0], half=1)


def line_gather(line, early, late, begin, more, use, even=False):
    gather = Gather(line, early + late, use, even)
    for piece in early:
        gather.start(piece)
    begin()
    for piece in late:
        gather.start(piece)
    more()

    @pl.loop(1, line.length + 1)
    def _(k):
        gather.step(k)

    gather.end()


def nothing(*_):
    pass


def gather_scratch(n):
    return [DMA((n // 2,)), DMA((2, n // 2)), DMA((n,)), DMA((2,))]


class Scatter:
    def __init__(self, line, items):
        self.line, self.items = line, items

    def over_x(self, item, a):
        _, _, x_out, x_in, _, _, _, send_x, recv_x = item[:9]
        return remote(x_out.at[a], x_in.at[a], send_x.at[a], recv_x.at[a], "dp", self.line.partner)

    def over_z(self, item, a, way, to=None):
        z_out, into, send, recv = item[4], item[5 + way], item[9], item[10 + way]
        return remote(z_out.at[a], into.at[a], send.at[a], recv.at[a], "dp", self.line.partner if to is None else to)

    def cross(self):
        length, at, side = self.line.length, self.line.at, self.line.side

        def one(a):
            for item in self.items:
                item[2][a] = item[0](a * 2 + 1 - side).astype(BF16)
                self.over_x(item, a).start()

        @pl.loop(0, length - 1)
        def _(step):
            k = length - 1 - step

            @pl.when(at + k < length)
            def _():
                one(at + k)

            @pl.when(at - k >= 0)
            def _():
                one(at - k)

        one(at)

    def relay(self, k):
        line = self.line
        length, at, side = line.length, line.at, line.side

        def one(a, way, behind, to):
            for item in self.items:
                make, _, _, x_in, z_out = item[:5]
                total = make(a * 2 + side)
                self.over_x(item, a).wait_recv()
                z_out[a] = (total + x_in[a].astype(F32)).astype(BF16)

                @pl.when(behind)
                def _():
                    self.over_z(item, a, way).wait_recv()
                    z_out[a] = (z_out[a].astype(F32) + item[5 + way][a].astype(F32)).astype(BF16)

                self.over_z(item, a, way, to).start()

        @pl.when(at + k < length)
        def _():
            one(at + k, 0, line.has_left, line.right)

        @pl.when(at - k >= 0)
        def _():
            one(at - k, 1, line.has_right, line.left)

    def end(self):
        line = self.line
        at = line.at
        for item in self.items:
            make, out, _, x_in, _, l_in, r_in = item[:7]
            total = make(line.place)
            self.over_x(item, at).wait_recv()
            out[...] = total + x_in[at].astype(F32)

            @pl.when(line.has_left)
            def _():
                self.over_z(item, at, 0).wait_recv()
                out[...] += l_in[at].astype(F32)

            @pl.when(line.has_right)
            def _():
                self.over_z(item, at, 1).wait_recv()
                out[...] += r_in[at].astype(F32)

        @pl.loop(0, line.length)
        def _(a):
            for item in self.items:
                self.over_x(item, a).wait_send()

            @pl.when(a != at)
            def _():
                for item in self.items:
                    self.over_z(item, a, 0).wait_send()


def line_scatter(line, items, middle):
    scatter = Scatter(line, items)
    scatter.cross()
    middle()

    @pl.loop(0, line.length - 1)
    def _(step):
        scatter.relay(line.length - 1 - step)

    scatter.end()


def scatter_scratch(n, shape):
    return [pltpu.VMEM((n // 2,) + shape, BF16)] * 5 + [DMA((n // 2,))] * 5


def gather_weights(arrays, corner, n):
    count = len(arrays)

    def kernel(*refs):
        owns, corner_ref, alls, part_ref = refs[:count], refs[count], refs[count + 1 : 2 * count + 1], refs[2 * count + 1]
        send, recv, kept_sem = refs[2 * count + 2 : 2 * count + 5]
        rest = refs[2 * count + 5 :]
        line = Line(n)
        place = line.place
        greet([("dp", n)])
        kept = [pltpu.make_async_copy(owns[i], alls[i].at[place], kept_sem.at[i]) for i in range(count)]

        def deal(s):
            return remote(corner_ref.at[s], part_ref, send.at[s], recv, "dp", s)

        def begin():
            for copy in kept:
                copy.start()

            @pl.when(place == 0)
            def _():
                @pl.loop(1, n)
                def _(s):
                    deal(s).start()

                part_ref[...] = corner_ref[0]

        pieces = [(owns[i], alls[i], *rest[4 * i : 4 * i + 4], nothing) for i in range(count)]
        line_gather(line, pieces, [], begin, nothing, nothing)
        for copy in kept:
            copy.wait()

        @pl.when(place != 0)
        def _():
            deal(0).wait_recv()

        @pl.when(place == 0)
        def _():
            @pl.loop(1, n)
            def _(s):
                deal(s).wait_send()

    return pl.pallas_call(
        kernel,
        in_specs=[ANY] * count + [INTO],
        out_specs=[ANY] * count + [INTO],
        out_shape=[jax.ShapeDtypeStruct((n,) + a.shape, a.dtype) for a in arrays]
        + [jax.ShapeDtypeStruct(corner.shape[1:], corner.dtype)],
        scratch_shapes=[DMA((n,)), DMA, DMA((count,))] + gather_scratch(n) * count,
        compiler_params=comm_params(0),
        name="gather_weights",
    )(*arrays, corner)


def swap(x, n, number, lanes_in=False, lanes_out=False):
    if lanes_in:
        block = (x.shape[0], x.shape[1] // n)
    else:
        block = x.shape[1:]
    shape = (block[0], n * block[1]) if lanes_out else (n,) + block

    def at(ref, lanes, j):
        if lanes:
            return ref.at[:, pl.ds(pl.multiple_of(j * block[1], block[1]), block[1])]
        return ref.at[j]

    def kernel(x_ref, out_ref, send, recv, own_sem):
        greet([("mp", n)])
        me = lax.axis_index("mp")
        copies = []
        for step in range(1, n):
            peer = lax.rem(me + step, n)
            copies.append(
                remote(at(x_ref, lanes_in, peer), at(out_ref, lanes_out, me), send.at[step], recv.at[step], "mp", peer)
            )
            copies[-1].start()
        own = pltpu.make_async_copy(at(x_ref, lanes_in, me), at(out_ref, lanes_out, me), own_sem)
        own.start()
        own.wait()
        for copy in copies:
            copy.wait()

    return pl.pallas_call(
        kernel,
        in_specs=[ANY],
        out_specs=ANY,
        out_shape=jax.ShapeDtypeStruct(shape, x.dtype),
        scratch_shapes=[DMA((n,)), DMA((n,)), DMA],
        compiler_params=comm_params(number),
        name="swap",
    )(x)


def table_forward(first, table, corner, parts, weights, n, n_mp):
    heads, rows, columns = table.shape
    _, width, share = parts.shape
    tokens = share * n_mp
    size = tokens - MOST
    owners = MOST // rows
    chunks = share // rows
    pairs = n_mp // 2

    def kernel(first_ref, table_ref, corner_ref, parts_ref, weights_ref, values_ref, mixed_ref, short_ref, lse_ref,
               all_ref, own, soft, sums, short_sum, v_send, v_recv, send_x, send_z, recv, more, send_m, recv_m, send_s,
               w_send_x, w_send_z, w_recv, w_more, w_own, far_send, far_recv, near_send, near_recv, on_send, on_recv):
        line = Line(n)
        place, me = line.place, lax.axis_index("mp")
        pair, core = me // 2, lax.rem(me, 2)
        twin = pair * 2 + 1 - core
        owner = place < owners
        greet_all(n, n_mp)

        def lanes(j):
            return own.at[:, pl.ds(pl.multiple_of(j * share, share), share)]

        gets = []
        for step in range(1, n_mp):
            peer = lax.rem(me + step, n_mp)
            gets.append(remote(parts_ref.at[peer], lanes(me), v_send.at[step], v_recv.at[step], "mp", peer))
        keep = pltpu.make_async_copy(weights_ref, all_ref.at[me, place], w_own)

        def prepare():
            offer(place, weights_ref)
            keep.start()
            own[:, pl.ds(pl.multiple_of(me * share, share), share)] = parts_ref[me]
            for copy in gets:
                copy.wait()
            values_ref[place] = own[:, 0:MOST]

        def over(step, s, source):
            to = lax.rem(pair + step, pairs) * 2 + core
            return remote(source, all_ref.at[me, s], far_send.at[step, s], far_recv.at[step, s], "mp", to)

        def across(s, source):
            return remote(source, all_ref.at[me, s], near_send.at[s], near_recv.at[s], "mp", twin)

        def onward(step, s):
            block = lax.rem(pair + pairs - step, pairs) * 2 + core
            return remote(
                all_ref.at[block, s], all_ref.at[block, s], on_send.at[step, s], on_recv.at[step, s], "mp", twin
            )

        def offer(s, source):
            for step in range(1, pairs):
                over(step, s, source).start()
            across(s, source).start()

        def product(s):
            for head in range(heads):
                span = slice(head * HD, (head + 1) * HD)
                sums[s, span, :] = nt(values_ref[s, span, :], soft[head]).astype(BF16)

        here = jnp.logical_and(owner, place // chunks == me)

        def back(s):
            return remote_to(
                sums.at[s],
                mixed_ref.at[me, lax.rem(place, chunks)],
                send_m.at[s],
                recv_m.at[me, lax.rem(place, chunks)],
                s,
                place // chunks,
            )

        def short_back():
            return remote(
                short_sum,
                mixed_ref.at[me, owners % chunks],
                send_s,
                recv_m.at[me, owners % chunks],
                "mp",
                owners // chunks,
            )

        def begin():
            short_ref[...] = own[:, MOST:tokens]
            for head in range(heads):
                scores = table_ref[head, :, 0:MOST].astype(F32)
                top = jnp.max(scores, axis=1, keepdims=True)
                powers = jnp.exp(scores - top)
                total = jnp.sum(powers, axis=1, keepdims=True)
                soft[head] = (powers / total).astype(BF16)
                lse_ref[head] = jnp.broadcast_to(top + jnp.log(total), (rows, 128))
            early, inside, shift, at = small_masks(first_ref[0, 0], size)
            for head in range(heads):
                span = slice(head * HD, (head + 1) * HD)
                weighed = by_token(masked_soft(nn(at, corner_ref[head]), inside), early, shift)
                short_sum[span, :] = nt(own[span, MOST:tokens], weighed).astype(BF16)

            @pl.when(me == owners // chunks)
            def _():
                mixed_ref[me, owners % chunks] = short_sum[...]

            @pl.when(me != owners // chunks)
            def _():
                short_back().start()

            @pl.when(owner)
            def _():
                product(place)

            @pl.when(here)
            def _():
                mixed_ref[me, lax.rem(place, chunks)] = sums[place]

            @pl.when(jnp.logical_and(owner, jnp.logical_not(here)))
            def _():
                back(place).start()

        def use(s):
            @pl.when(owner)
            def _():
                product(s)
                back(s).start()

        for copy in gets:
            copy.start()
        line_gather(
            line,
            [(weights_ref, all_ref.at[me], w_send_x, w_send_z, w_recv, w_more, lambda s: offer(s, all_ref.at[me, s]))],
            [(values_ref.at[place], values_ref, send_x, send_z, recv, more, nothing)],
            prepare,
            begin,
            use,
            even=True,
        )

        @pl.loop(0, n)
        def _(s):
            for step in range(1, pairs):
                over(step, s, weights_ref).wait_recv()
                onward(step, s).start()

        @pl.loop(0, n)
        def _(s):
            @pl.when(jnp.logical_and(owner, jnp.logical_or(s != place, jnp.logical_not(here))))
            def _():
                back(s).wait_send()

            across(s, weights_ref).wait()
            for step in range(1, pairs):
                over(step, s, weights_ref).wait_send()
                onward(step, s).wait()

        @pl.when(me != owners // chunks)
        def _():
            short_back().wait_send()

        for c in range(chunks):
            d = me * chunks + c
            for g in range(n_mp):
                source = jnp.where(d < owners, d, place)

                @pl.when(jnp.logical_not(jnp.logical_and(source == place, g == me)))
                def _():
                    remote(short_sum, mixed_ref.at[g, c], send_s, recv_m.at[g, c], "mp", twin).wait_recv()

        keep.wait()

    return pl.pallas_call(
        kernel,
        in_specs=[SCALAR, INTO, INTO, INTO, ANY],
        out_specs=[INTO, INTO, INTO, INTO, ANY],
        out_shape=[
            jax.ShapeDtypeStruct((n, width, MOST), BF16),
            jax.ShapeDtypeStruct((n_mp, chunks, width, rows), BF16),
            jax.ShapeDtypeStruct((width, size), BF16),
            jax.ShapeDtypeStruct((heads, rows, 128), F32),
            jax.ShapeDtypeStruct((n_mp, n) + weights.shape, BF16),
        ],
        scratch_shapes=[
            pltpu.VMEM((width, tokens), BF16),
            pltpu.VMEM((heads, rows, MOST), BF16),
            pltpu.VMEM((n, width, rows), BF16),
            pltpu.VMEM((width, rows), BF16),
            DMA((n_mp,)),
            DMA((n_mp,)),
            *gather_scratch(n),
            DMA((n,)),
            DMA((n_mp, chunks)),
            DMA,
            *gather_scratch(n),
            DMA,
            DMA((pairs, n)),
            DMA((pairs, n)),
            DMA((n,)),
            DMA((n,)),
            DMA((pairs, n)),
            DMA((pairs, n)),
        ],
        compiler_params=comm_params(1),
        name="table_forward",
    )(first, table, corner, parts, weights)


def spread_mp(x_ref, all_ref, send, recv, own_sem, n):
    me, pairs = lax.axis_index("mp"), n // 2
    pair, core = me // 2, lax.rem(me, 2)
    twin = pair * 2 + 1 - core
    own = pltpu.make_async_copy(x_ref, all_ref.at[me], own_sem)
    near = remote(x_ref, all_ref.at[me], send.at[0], recv.at[0], "mp", twin)

    def far(step):
        to = lax.rem(pair + step, pairs) * 2 + core
        return remote(x_ref, all_ref.at[me], send.at[step], recv.at[step], "mp", to)

    def onward(step):
        source = lax.rem(pair + pairs - step, pairs) * 2 + core
        return remote(
            all_ref.at[source], all_ref.at[source], send.at[pairs + step], recv.at[pairs + step], "mp", twin
        )

    def start():
        for step in range(1, pairs):
            far(step).start()
        near.start()
        own.start()

    def relay():
        for step in range(1, pairs):
            far(step).wait_recv()
            onward(step).start()

    def end():
        for step in range(1, pairs):
            far(step).wait_send()
            onward(step).wait()
        near.wait()
        own.wait()

    return start, relay, end


def blend_mp(x_ref, out_refs, kept, twins, others, local, near_send, near_recv, far_send, far_recv, n):
    me, pairs = lax.axis_index("mp"), n // 2
    pair, core = me // 2, lax.rem(me, 2)
    twin = pair * 2 + 1 - core
    rows = x_ref.shape[1]
    chunk = rows // 6

    def keep(p):
        return pltpu.make_async_copy(x_ref.at[p * 2 + core], kept.at[p], local.at[p])

    def give(p):
        return remote(x_ref.at[p * 2 + 1 - core], twins.at[p], near_send.at[p], near_recv.at[p], "mp", twin)

    def pass_on(step):
        to = lax.rem(pair + step, pairs)
        return remote(
            kept.at[to], others.at[step - 1], far_send.at[step], far_recv.at[step], "mp", to * 2 + core
        )

    def over_rows(body):
        @pl.loop(0, rows // chunk)
        def _(i):
            body(pl.ds(pl.multiple_of(i * chunk, chunk), chunk))

    def start():
        for step in range(1, pairs + 1):
            p = lax.rem(pair + step, pairs)
            give(p).start()
            keep(p).start()

    def go_on():
        for step in range(1, pairs):
            p = lax.rem(pair + step, pairs)
            keep(p).wait()
            give(p).wait_recv()

            def body(at):
                kept[p, at, :] = (kept[p, at, :].astype(F32) + twins[p, at, :].astype(F32)).astype(BF16)

            over_rows(body)
            pass_on(step).start()

    def end():
        keep(pair).wait()
        give(pair).wait_recv()
        for step in range(1, pairs):
            pass_on(step).wait_recv()

        def body(at):
            total = kept[pair, at, :].astype(F32) + twins[pair, at, :].astype(F32)
            for j in range(pairs - 1):
                total += others[j, at, :].astype(F32)
            spot = 0
            for ref in out_refs:
                ref[at, :] = total[:, spot : spot + ref.shape[1]].astype(BF16)
                spot += ref.shape[1]

        over_rows(body)
        for p in range(pairs):
            give(p).wait_send()
        for step in range(1, pairs):
            pass_on(step).wait_send()

    return start, go_on, end


def blend_scratch(n, shape):
    pairs = n // 2
    return [
        pltpu.VMEM((pairs,) + shape, BF16),
        pltpu.VMEM((pairs,) + shape, BF16),
        pltpu.VMEM((pairs - 1,) + shape, BF16),
    ] + [DMA((pairs,))] * 5


def table_backward(first, table, corner, lse, short_t, parts, grads, n, n_mp):
    heads, rows, columns = table.shape
    width, size = short_t.shape
    owners = MOST // rows
    _, chunks, _, _ = parts.shape
    share = chunks * rows

    def kernel(first_ref, table_ref, corner_ref, lse_ref, short_ref, parts_ref, grads_ref, ups, got_ref, dcorner_ref,
               blended_ref, full, short_up, total, soft, send_u, recv_u, recv_s, v_send, v_recv, *rest):
        line = Line(n)
        place, me = line.place, lax.axis_index("mp")
        owner = place < owners
        greet_all(n, n_mp)
        blend, go_on, blended = blend_mp(grads_ref, [blended_ref], *rest[10:], n_mp)

        def hand(g, c):
            return remote_to(
                parts_ref.at[g, c], ups.at[place], send_u.at[g, c], recv_u.at[place], me * chunks + c, g
            )

        def hand_short(g, c):
            return remote_to(parts_ref.at[g, c], short_up, send_u.at[g, c], recv_s, place, g)

        def each_hand(act):
            for c in range(chunks):
                d = me * chunks + c
                for g in range(n_mp):
                    @pl.when(jnp.logical_and(d < owners, jnp.logical_not(jnp.logical_and(d == place, g == me))))
                    def _():
                        act(hand(g, c))

                    @pl.when(jnp.logical_and(d == owners, g != me))
                    def _():
                        act(hand_short(g, c))

        each_hand(lambda copy: copy.start())
        blend()

        @pl.when(jnp.logical_and(owner, place // chunks == me))
        def _():
            ups[place] = parts_ref[me, lax.rem(place, chunks)]

        @pl.when(me == owners // chunks)
        def _():
            short_up[...] = parts_ref[me, owners % chunks]

        for head in range(heads):
            soft[head] = jnp.exp(table_ref[head, :, 0:MOST].astype(F32) - lse_ref[head, :, 0:1]).astype(BF16)

        @pl.when(me != owners // chunks)
        def _():
            hand_short(0, 0).wait_recv()

        early, inside, shift, at = small_masks(first_ref[0, 0], size)
        for head in range(heads):
            span = slice(head * HD, (head + 1) * HD)
            weights = masked_soft(nn(at, corner_ref[head]), inside)
            here, up = short_ref[span, :], short_up[span, :]
            moved = nt(here, shift).astype(BF16)
            dsoft = jnp.where(early, tn(up, here), tn(up, moved))
            full[span, MOST : MOST + size] = nn(up, by_token(weights, early, shift)).astype(BF16)
            centre = jnp.sum(weights * dsoft, axis=1, keepdims=True)
            dcorner_ref[head] = tn(at, (weights * (dsoft - centre)).astype(BF16)).astype(BF16)

        def make(s):
            @pl.when(jnp.logical_and(owner, jnp.logical_not(jnp.logical_and(s == place, place // chunks == me))))
            def _():
                remote(short_up, ups.at[s], send_u.at[0, 0], recv_u.at[s], "dp", line.partner).wait_recv()

            @pl.when(jnp.logical_not(owner))
            def _():
                ups[s] = jnp.zeros((width, rows), BF16)

            return jnp.concatenate(
                [nn(ups[s, head * HD : (head + 1) * HD, :], soft[head]) for head in range(heads)], axis=0
            )

        line_scatter(line, [(make, total, *rest[:10])], go_on)
        full[:, 0:MOST] = total[...].astype(BF16)

        def lanes(j):
            return full.at[:, pl.ds(pl.multiple_of(j * share, share), share)]

        gives = []
        for step in range(1, n_mp):
            peer = lax.rem(me + step, n_mp)
            gives.append(remote(lanes(peer), got_ref.at[me], v_send.at[step], v_recv.at[step], "mp", peer))
            gives[-1].start()
        got_ref[me] = full[:, pl.ds(pl.multiple_of(me * share, share), share)]
        blended()
        each_hand(lambda copy: copy.wait_send())
        for copy in gives:
            copy.wait()

    return pl.pallas_call(
        kernel,
        in_specs=[SCALAR] + [INTO] * 5 + [ANY],
        out_specs=[INTO] * 4,
        out_shape=[
            jax.ShapeDtypeStruct((n, width, rows), BF16),
            jax.ShapeDtypeStruct((n_mp, width, share), BF16),
            jax.ShapeDtypeStruct((heads, size, size), BF16),
            jax.ShapeDtypeStruct(grads.shape[1:], BF16),
        ],
        scratch_shapes=[
            pltpu.VMEM((width, share * n_mp), BF16),
            pltpu.VMEM((width, rows), BF16),
            pltpu.VMEM((width, MOST), F32),
            pltpu.VMEM((heads, rows, MOST), BF16),
            DMA((n_mp, chunks)),
            DMA((n,)),
            DMA,
            DMA((n_mp,)),
            DMA((n_mp,)),
        ]
        + scatter_scratch(n, (width, MOST))
        + blend_scratch(n_mp, grads.shape[1:]),
        compiler_params=comm_params(2),
        name="table_backward",
    )(first, table, corner, lse, short_t, parts, grads)


def last_exchange(back, grads, n, n_mp):
    count = len(grads)

    def kernel(*refs):
        back_ref, grad_refs = refs[0], refs[1 : 1 + count]
        got_ref, out_refs = refs[1 + count], refs[2 + count : 2 + 2 * count]
        send, recv, own_sem, part, part_send, part_recv, last = refs[2 + 2 * count : 9 + 2 * count]
        rest = refs[9 + 2 * count :]
        line = Line(n)
        place, me = line.place, lax.axis_index("mp")
        greet([("dp", n), ("mp", n_mp)])
        copies = []
        for step in range(1, n_mp):
            peer = lax.rem(me + step, n_mp)
            copies.append(
                remote(back_ref.at[peer], got_ref.at[me], send.at[step], recv.at[step], "mp", peer)
            )
            copies[-1].start()
        own = pltpu.make_async_copy(back_ref.at[me], got_ref.at[me], own_sem)
        own.start()
        outs = [*out_refs[: count - 1], last]
        items = [
            (lambda s, ref=grad_refs[i]: ref[s].astype(F32), outs[i], *rest[10 * i : 10 * i + 10])
            for i in range(count)
        ]
        line_scatter(line, items, nothing)
        part[...] = last[...].astype(BF16)

        def hand(s):
            return remote(part, out_refs[-1].at[s], part_send, part_recv.at[s], "dp", 0)

        @pl.when(place != 0)
        def _():
            hand(place).start()
            hand(place).wait_send()

        @pl.when(place == 0)
        def _():
            out_refs[-1][0] = part[...]

            @pl.loop(1, n)
            def _(s):
                hand(s).wait_recv()

        @pl.when(place != 0)
        def _():
            out_refs[-1][...] = jnp.zeros_like(out_refs[-1])

        own.wait()
        for copy in copies:
            copy.wait()

    return pl.pallas_call(
        kernel,
        in_specs=[ANY] + [INTO] * count,
        out_specs=[ANY] + [INTO] * count,
        out_shape=[jax.ShapeDtypeStruct(back.shape, BF16)]
        + [jax.ShapeDtypeStruct(g.shape[1:], F32) for g in grads[:-1]]
        + [jax.ShapeDtypeStruct(grads[-1].shape, BF16)],
        scratch_shapes=[DMA((n_mp,)), DMA((n_mp,)), DMA]
        + [pltpu.VMEM(grads[-1].shape[1:], BF16), DMA, DMA((n,)), pltpu.VMEM(grads[-1].shape[1:], F32)]
        + [each for g in grads for each in scatter_scratch(n, g.shape[1:])],
        compiler_params=comm_params(3),
        name="last_exchange",
    )(back, *grads)


def nn(a, b):
    return lax.dot_general(a, b, (((1,), (0,)), ((), ())), preferred_element_type=F32)


def nt(a, b):
    return lax.dot_general(a, b, (((1,), (1,)), ((), ())), preferred_element_type=F32)


def tn(a, b):
    return lax.dot_general(a, b, (((0,), (0,)), ((), ())), preferred_element_type=F32)


def small_masks(first, size):
    row = lax.broadcasted_iota(jnp.int32, (size, size), 0)
    col = lax.broadcasted_iota(jnp.int32, (size, size), 1)
    early = row < first
    inside = col < jnp.where(early, first, size - first)
    shift = jnp.where(col == row + first, 1.0, 0.0).astype(BF16)
    rows = jnp.where(col == jnp.where(early, row, row - first), 1.0, 0.0).astype(BF16)
    return early, inside, shift, rows


def masked_soft(scores, inside):
    masked = jnp.where(inside, scores, -1e30)
    powers = jnp.where(inside, jnp.exp(masked - jnp.max(masked, axis=1, keepdims=True)), 0.0)
    return powers / jnp.sum(powers, axis=1, keepdims=True)


def by_token(soft, early, shift):
    low = soft.astype(BF16)
    zero = jnp.zeros_like(low)
    late = nn(jnp.where(early, zero, low), shift).astype(BF16)
    return jnp.where(early, low, zero) + late


def dense_forward(first, acts, values, table, part=None, n=None, n_mp=None):
    busy = part is not None
    tokens, width = acts.shape
    heads = width // HD
    tiles = MOST // TILE
    size = tokens - MOST
    columns = table.shape[2]
    blocks = MOST // columns

    def kernel(first_ref, acts_ref, values_ref, table_ref, *refs):
        tile = pl.program_id(0)
        if busy:
            part_ref, got_ref, lse_ref, all_ref, out_ref, give_send, give_recv, own_sem, *rest = refs
            line = Line(n)
            me = lax.axis_index("mp")
            share = tokens // n_mp
            piece = (part_ref, all_ref, *rest, nothing)
            gather = Gather(line, [piece], nothing)

            @pl.when(tile == 0)
            def _():
                pltpu.make_async_copy(part_ref, all_ref.at[line.place], own_sem.at[0]).start()
                greet([("dp", n), ("mp", n_mp)])
                gather.start(piece)

            for k in range(1, line.length + 1):
                @pl.when(tile == min(2 * k, tiles))
                def _():
                    gather.step(k)

            def give(j):
                rows = out_ref.at[pl.ds(j * share, share)]
                return remote(rows, got_ref.at[me], give_send.at[j], give_recv.at[me], "mp", j)

            def keep():
                rows = out_ref.at[pl.ds(pl.multiple_of(me * share, share), share)]
                return pltpu.make_async_copy(rows, got_ref.at[me], own_sem.at[1])

            def put(rows):
                out_ref[pl.ds(pl.multiple_of(tile * TILE, TILE), TILE), :] = rows
                for j in range(n_mp):
                    done = tile == (j + 1) * share // TILE - 1

                    @pl.when(jnp.logical_and(done, me == j))
                    def _():
                        keep().start()

                    @pl.when(jnp.logical_and(done, me != j))
                    def _():
                        give(j).start()
        else:
            out_ref, lse_ref = refs

            def put(rows):
                out_ref[...] = rows
        lane = lax.broadcasted_iota(jnp.int32, (TILE, 128), 1)

        def scored(span, number):
            parts = [nn(acts_ref[:, span], table_ref[b, span, :]) for b in range(number)]
            return jnp.concatenate(parts, axis=1)

        @pl.when(tile < tiles)
        def _():
            lse = jnp.zeros((TILE, 128), F32)
            parts = []
            spans = [slice(head * HD, (head + 1) * HD) for head in range(heads)]
            ahead = scored(spans[0], blocks)
            for head in range(heads):
                scores = ahead
                if head + 1 < heads:
                    ahead = scored(spans[head + 1], blocks)
                top = jnp.max(scores, axis=1, keepdims=True)
                powers = jnp.exp(scores - top)
                total = jnp.sum(powers, axis=1, keepdims=True)
                mixed = nn(powers.astype(BF16), values_ref[0:MOST, spans[head]])
                parts.append((mixed / total).astype(BF16))
                lse = jnp.where(lane == head, top + jnp.log(total), lse)
            put(jnp.concatenate(parts, axis=1))
            lse_ref[...] = lse

        @pl.when(tile == tiles)
        def _():
            early, inside, shift, _ = small_masks(first_ref[0, 0], size)
            parts = []
            for head in range(heads):
                span = slice(head * HD, (head + 1) * HD)
                soft = by_token(masked_soft(scored(span, size // columns), inside), early, shift)
                parts.append(nn(soft, values_ref[MOST:tokens, span]).astype(BF16))
            put(jnp.concatenate(parts, axis=1))
            lse_ref[...] = jnp.zeros((TILE, 128), F32)
            if busy:
                gather.end()
                keep().wait()
                pltpu.make_async_copy(part_ref, all_ref.at[line.place], own_sem.at[0]).wait()
                for j in range(n_mp):
                    @pl.when(me != j)
                    def _():
                        give(j).wait_send()
                        remote(out_ref.at[0:share], got_ref.at[j], give_send.at[j], give_recv.at[j], "mp", j).wait_recv()

    return pl.pallas_call(
        kernel,
        grid=(tiles + 1,),
        in_specs=[
            pl.BlockSpec(memory_space=pltpu.SMEM),
            pl.BlockSpec((TILE, width), lambda t: (t, 0)),
            pl.BlockSpec((tokens, width), lambda t: (0, 0)),
            pl.BlockSpec(table.shape, lambda t: (0, 0, 0)),
        ]
        + [ANY] * busy,
        out_specs=[
            ANY if busy else pl.BlockSpec((TILE, width), lambda t: (t, 0)),
            pl.BlockSpec((TILE, 128), lambda t: (t, 0)),
        ]
        + [ANY] * busy,
        out_shape=[
            jax.ShapeDtypeStruct((n_mp, tokens // n_mp, width) if busy else (tokens, width), BF16),
            jax.ShapeDtypeStruct((tokens, 128), F32),
        ]
        + ([jax.ShapeDtypeStruct((n,) + part.shape, part.dtype)] if busy else []),
        scratch_shapes=[pltpu.VMEM((tokens, width), BF16), DMA((n_mp,)), DMA((n_mp,)), DMA((2,))] + gather_scratch(n) if busy else [],
        compiler_params=comm_params(8) if busy else pltpu.CompilerParams(vmem_limit_bytes=VMEM),
        cost_estimate=pl.CostEstimate(flops=12 * tokens * tokens * width, bytes_accessed=8 * tokens * width, transcendentals=0),
        name="dense_forward",
    )(first, acts, values, table, *([part] if busy else []))


def dense_backward(first, acts, acts_t, values_t, upstream, table, lse, slope, normed, parts=None, give=None, n=None, n_mp=None):
    busy = parts is not None
    tokens, width = acts.shape
    model = normed.shape[1]
    heads = width // HD
    tiles = MOST // TILE
    size = tokens - MOST
    columns = table.shape[2]
    blocks = MOST // columns

    def kernel(first_ref, acts_ref, acts_t_ref, values_t_ref, up_ref, table_ref, lse_ref, slope_ref, normed_ref, *refs):
        tile = pl.program_id(0)
        if busy:
            parts_ref, give_ref, back_ref, dweights_ref, dtable_ref, part_ref, all_ref = refs[:7]
            dv_acc, dt_acc, dpre, send, recv, own_sem, *rest = refs[7:]
            line = Line(n)
            scatter = Scatter(line, [(lambda s: parts_ref[s].astype(F32), part_ref, *rest)])
            start, relay, end = spread_mp(give_ref, all_ref, send, recv, own_sem, n_mp)

            @pl.when(tile == 0)
            def _():
                greet([("dp", n), ("mp", n_mp)])
                start()
                scatter.cross()

            for k in range(line.length - 1, 0, -1):
                @pl.when(tile == 2 * (line.length - k))
                def _():
                    scatter.relay(k)

            @pl.when(tile == 5)
            def _():
                relay()
        else:
            back_ref, dweights_ref, dtable_ref, dv_acc, dt_acc, dpre = refs

        @pl.when(tile == 0)
        def _():
            dv_acc[...] = jnp.zeros_like(dv_acc)
            dt_acc[...] = jnp.zeros_like(dt_acc)

        def scored(span, number):
            parts = [nn(acts_ref[:, span], table_ref[b, span, :]) for b in range(number)]
            return jnp.concatenate(parts, axis=1)

        def spread(span, dscores, number):
            total = 0.0
            for b in range(number):
                part = dscores[:, b * columns : (b + 1) * columns]
                dt_acc[b, span, :] += nn(acts_t_ref[span, :], part)
                total += nt(part, table_ref[b, span, :])
            return total

        def keep(parts):
            slopes = slope_ref[...].astype(F32)
            rows = pl.ds(pl.multiple_of(tile * TILE, TILE), TILE)
            dpre[rows, :] = (slopes * jnp.concatenate(parts, axis=1)).astype(BF16)

        @pl.when(tile < tiles)
        def _():
            parts = []
            up_t = up_ref[...].T
            spans = [slice(head * HD, (head + 1) * HD) for head in range(heads)]

            def made(span):
                return scored(span, blocks), nn(up_ref[:, span], values_t_ref[span, 0:MOST])

            ahead = made(spans[0])
            for head in range(heads):
                span = spans[head]
                scores, dsoft = ahead
                if head + 1 < heads:
                    ahead = made(spans[head + 1])
                soft = jnp.exp(scores - lse_ref[:, head : head + 1])
                dv_acc[span, 0:MOST] += nn(up_t[span, :], soft.astype(BF16))
                weighed = soft * dsoft
                centre = jnp.sum(weighed, axis=1, keepdims=True)
                parts.append(spread(span, (soft * (dsoft - centre)).astype(BF16), blocks))
            keep(parts)

        @pl.when(tile == tiles)
        def _():
            early, inside, shift, _ = small_masks(first_ref[0, 0], size)
            parts = []
            up_t = up_ref[...].T
            for head in range(heads):
                span = slice(head * HD, (head + 1) * HD)
                soft = masked_soft(scored(span, size // columns), inside)
                here = values_t_ref[span, MOST:tokens]
                moved = nt(here, shift).astype(BF16)
                dsoft = jnp.where(early, nn(up_ref[:, span], here), nn(up_ref[:, span], moved))
                dv_acc[span, MOST:tokens] = nn(up_t[span, :], by_token(soft, early, shift))
                centre = jnp.sum(soft * dsoft, axis=1, keepdims=True)
                parts.append(spread(span, (soft * (dsoft - centre)).astype(BF16), size // columns))
            keep(parts)
            dvalues_t = dv_acc[...].astype(BF16)
            back_ref[:, 0:width] = dvalues_t.T
            back_ref[:, width:] = dpre[...]
            value_grad = nn(dvalues_t, normed_ref[...])
            first_grad = nn(dpre[...].T, normed_ref[...])
            dweights_ref[:, 0:width] = value_grad.T.astype(BF16)
            dweights_ref[:, width:] = first_grad.T.astype(BF16)
            dtable_ref[...] = dt_acc[...].astype(BF16)
            if busy:
                scatter.end()
                end()

    whole = lambda t: (0, 0)
    rows = lambda t: (t, 0)
    return pl.pallas_call(
        kernel,
        grid=(tiles + 1,),
        in_specs=[
            pl.BlockSpec(memory_space=pltpu.SMEM),
            pl.BlockSpec((TILE, width), rows),
            pl.BlockSpec((width, TILE), lambda t: (0, t)),
            pl.BlockSpec((width, tokens), whole),
            pl.BlockSpec((TILE, width), rows),
            pl.BlockSpec(table.shape, lambda t: (0, 0, 0)),
            pl.BlockSpec((TILE, 128), rows),
            pl.BlockSpec((TILE, width), rows),
            pl.BlockSpec((tokens, model), whole),
        ]
        + [INTO, ANY] * busy,
        out_specs=[
            pl.BlockSpec((tokens, 2 * width), whole),
            pl.BlockSpec((model, 2 * width), whole),
            pl.BlockSpec(table.shape, lambda t: (0, 0, 0)),
        ]
        + [INTO, ANY] * busy,
        out_shape=[
            jax.ShapeDtypeStruct((tokens, 2 * width), BF16),
            jax.ShapeDtypeStruct((model, 2 * width), BF16),
            jax.ShapeDtypeStruct(table.shape, BF16),
        ]
        + (
            [
                jax.ShapeDtypeStruct(parts.shape[1:], F32),
                jax.ShapeDtypeStruct((n_mp,) + give.shape, give.dtype),
            ]
            if busy
            else []
        ),
        scratch_shapes=[
            pltpu.VMEM((width, tokens), F32),
            pltpu.VMEM(table.shape, F32),
            pltpu.VMEM((tokens, width), BF16),
        ]
        + ([DMA((n_mp,)), DMA((n_mp,)), DMA] + scatter_scratch(n, parts.shape[1:]) if busy else []),
        compiler_params=comm_params(9) if busy else pltpu.CompilerParams(vmem_limit_bytes=VMEM),
        cost_estimate=pl.CostEstimate(flops=24 * tokens * tokens * width, bytes_accessed=16 * tokens * width, transcendentals=0),
        name="dense_backward",
    )(first, acts, acts_t, values_t, upstream, table, lse, slope, normed, *([parts, give] if busy else []))


def random_forward(table, values_t):
    heads, rows, _ = table.shape
    slots, width, _ = values_t.shape

    def kernel(table_ref, values_ref, out_ref, lse_ref):
        scores = table_ref[0, :, 0:MOST].astype(F32)
        top = jnp.max(scores, axis=1, keepdims=True)
        powers = jnp.exp(scores - top)
        total = jnp.sum(powers, axis=1, keepdims=True)
        soft = (powers / total).astype(BF16)
        values = values_ref[...].reshape(slots * HD, MOST)
        out_ref[...] = nt(values, soft).astype(BF16).reshape(slots, HD, rows)
        lse_ref[...] = jnp.broadcast_to(top + jnp.log(total), (1, rows, 128))

    return pl.pallas_call(
        kernel,
        grid=(heads,),
        in_specs=[
            pl.BlockSpec((1, rows, table.shape[2]), lambda h: (h, 0, 0)),
            pl.BlockSpec((slots, HD, MOST), lambda h: (0, h, 0)),
        ],
        out_specs=[
            pl.BlockSpec((slots, HD, rows), lambda h: (0, h, 0)),
            pl.BlockSpec((1, rows, 128), lambda h: (h, 0, 0)),
        ],
        out_shape=[
            jax.ShapeDtypeStruct((slots, width, rows), BF16),
            jax.ShapeDtypeStruct((heads, rows, 128), F32),
        ],
        compiler_params=pltpu.CompilerParams(vmem_limit_bytes=VMEM),
        name="random_forward",
    )(table, values_t)


def random_backward(valid, table, lse, values_t, upstream_t):
    heads, rows, columns = table.shape
    slots, width, _ = values_t.shape
    buffers = pl.Buffered(2 if slots <= 16 else 1)

    def kernel(valid_ref, table_ref, lse_ref, values_ref, up_ref, dtable_ref, dvalues_ref):
        soft = jnp.exp(table_ref[0, :, 0:MOST].astype(F32) - lse_ref[0, :, 0:1])
        up = up_ref[...].reshape(slots * HD, rows) * valid_ref[0, 0].astype(BF16)
        values = values_ref[...].reshape(slots * HD, MOST)
        dsoft = tn(up, values)
        weighed = soft * dsoft
        centre = jnp.sum(weighed, axis=1, keepdims=True)
        dtable_ref[0, :, 0:MOST] = weighed - soft * centre
        dtable_ref[0, :, MOST:columns] = jnp.zeros((rows, columns - MOST), F32)
        dvalues_ref[...] = nn(up, soft.astype(BF16)).astype(BF16).reshape(slots, HD, MOST)

    return pl.pallas_call(
        kernel,
        grid=(heads,),
        in_specs=[
            pl.BlockSpec(memory_space=pltpu.SMEM),
            pl.BlockSpec((1, rows, columns), lambda h: (h, 0, 0)),
            pl.BlockSpec((1, rows, 128), lambda h: (h, 0, 0)),
            pl.BlockSpec((slots, HD, MOST), lambda h: (0, h, 0), pipeline_mode=buffers),
            pl.BlockSpec((slots, HD, rows), lambda h: (0, h, 0)),
        ],
        out_specs=[
            pl.BlockSpec((1, rows, columns), lambda h: (h, 0, 0)),
            pl.BlockSpec((slots, HD, MOST), lambda h: (0, h, 0)),
        ],
        out_shape=[
            jax.ShapeDtypeStruct((heads, rows, columns), F32),
            jax.ShapeDtypeStruct((slots, width, MOST), BF16),
        ],
        compiler_params=pltpu.CompilerParams(vmem_limit_bytes=VMEM),
        name="random_backward",
    )(valid, table, lse, values_t, upstream_t)


def short_forward(first, corner, values_t):
    heads, size, _ = corner.shape
    width = values_t.shape[0]

    def kernel(first_ref, corner_ref, values_ref, out_ref):
        early, inside, shift, rows = small_masks(first_ref[0, 0], size)
        for head in range(heads):
            span = slice(head * HD, (head + 1) * HD)
            soft = by_token(masked_soft(nn(rows, corner_ref[head]), inside), early, shift)
            out_ref[span, :] = nt(values_ref[span, :], soft).astype(BF16)

    return pl.pallas_call(
        kernel,
        in_specs=[
            pl.BlockSpec(memory_space=pltpu.SMEM),
            pl.BlockSpec(memory_space=pltpu.VMEM),
            pl.BlockSpec(memory_space=pltpu.VMEM),
        ],
        out_specs=pl.BlockSpec(memory_space=pltpu.VMEM),
        out_shape=jax.ShapeDtypeStruct((width, size), BF16),
        name="short_forward",
    )(first, corner, values_t)


def short_backward(first, corner, values_t, upstream_t):
    heads, size, _ = corner.shape
    width = values_t.shape[0]

    def kernel(first_ref, corner_ref, values_ref, up_ref, dcorner_ref, dvalues_ref):
        early, inside, shift, rows = small_masks(first_ref[0, 0], size)
        for head in range(heads):
            span = slice(head * HD, (head + 1) * HD)
            soft = masked_soft(nn(rows, corner_ref[head]), inside)
            here, up = values_ref[span, :], up_ref[span, :]
            moved = nt(here, shift).astype(BF16)
            dsoft = jnp.where(early, tn(up, here), tn(up, moved))
            dvalues_ref[span, :] = nn(up, by_token(soft, early, shift)).astype(BF16)
            centre = jnp.sum(soft * dsoft, axis=1, keepdims=True)
            dscores = (soft * (dsoft - centre)).astype(BF16)
            dcorner_ref[head] = tn(rows, dscores).astype(BF16)

    return pl.pallas_call(
        kernel,
        in_specs=[
            pl.BlockSpec(memory_space=pltpu.SMEM),
            pl.BlockSpec(memory_space=pltpu.VMEM),
            pl.BlockSpec(memory_space=pltpu.VMEM),
            pl.BlockSpec(memory_space=pltpu.VMEM),
        ],
        out_specs=[
            pl.BlockSpec(memory_space=pltpu.VMEM),
            pl.BlockSpec(memory_space=pltpu.VMEM),
        ],
        out_shape=[
            jax.ShapeDtypeStruct((heads, size, size), BF16),
            jax.ShapeDtypeStruct((width, size), BF16),
        ],
        name="short_backward",
    )(first, corner, values_t, upstream_t)


def table_grad(table, lse, values_t, upstream_t, corner):
    heads, rows, columns = table.shape
    slots, size = values_t.shape[0], corner.shape[2]

    def kernel(table_ref, lse_ref, values_ref, up_ref, corner_ref, out_ref):
        weights = jnp.exp(table_ref[0, :, 0:MOST].astype(F32) - lse_ref[0, :, 0:1])
        up = up_ref[...].reshape(slots * HD, rows)
        dsoft = tn(up, values_ref[...].reshape(slots * HD, MOST))
        weighed = weights * dsoft
        centre = jnp.sum(weighed, axis=1, keepdims=True)
        out_ref[0, :, 0:MOST] = weighed - weights * centre
        out_ref[0, :, MOST:columns] = jnp.zeros((rows, columns - MOST), F32)
        out_ref[0, :, 0:size] += corner_ref[0].astype(F32)

    return pl.pallas_call(
        kernel,
        grid=(heads,),
        in_specs=[
            pl.BlockSpec((1, rows, columns), lambda h: (h, 0, 0)),
            pl.BlockSpec((1, rows, 128), lambda h: (h, 0, 0)),
            pl.BlockSpec((slots, HD, MOST), lambda h: (0, h, 0)),
            pl.BlockSpec((slots, HD, rows), lambda h: (0, h, 0)),
            pl.BlockSpec((1, rows, size), lambda h: (h, 0, 0)),
        ],
        out_specs=pl.BlockSpec((1, rows, columns), lambda h: (h, 0, 0)),
        out_shape=jax.ShapeDtypeStruct((heads, rows, columns), F32),
        compiler_params=pltpu.CompilerParams(vmem_limit_bytes=VMEM),
        name="table_grad",
    )(table, lse, values_t, upstream_t, corner)


EPS = 1e-06
CURVE = 0.7978845608028654


def root(x):
    return lax.rsqrt(jnp.mean(x * x, axis=-1, keepdims=True) + EPS)


def normalize(x, gain):
    return (x * root(x) * gain).astype(BF16)


def normalize_back(x, gain, grad):
    scale = root(x)
    weighed = grad * gain
    pull = jnp.mean(weighed * x, axis=-1, keepdims=True)
    return scale * weighed - x * (scale * scale * scale * pull), jnp.sum(grad * x * scale, axis=0, keepdims=True)


def gelu(x):
    square = x * x
    half = 0.5 * jnp.tanh(x * (CURVE + CURVE * 0.044715 * square)) + 0.5
    value = x * half
    return value, half + (value - value * half) * (2 * CURVE + 6 * CURVE * 0.044715 * square)


def turn(x, start, rows):
    total, model = x.shape

    def kernel(start_ref, x_ref, out_ref, wide):
        for i in range(model // 128):
            lanes = slice(i * 128, (i + 1) * 128)
            part = x_ref[:, lanes].astype(F32)
            wide[i % 2, 0:total] = part
            wide[i % 2, total : total + rows] = part[0:rows]
            out_ref[:, lanes] = wide[i % 2, pl.ds(start_ref[0, 0], rows), :].astype(x.dtype)

    return pl.pallas_call(
        kernel,
        in_specs=[SCALAR, INTO],
        out_specs=INTO,
        out_shape=jax.ShapeDtypeStruct((rows, model), x.dtype),
        scratch_shapes=[pltpu.VMEM((2, total + rows, 128), F32)],
        compiler_params=pltpu.CompilerParams(vmem_limit_bytes=VMEM),
        name="turn",
    )(start.astype(jnp.int32).reshape(1, 1), x)


def begin(inputs, weights, gain):
    total, model = inputs.shape
    width = weights.shape[1] // 2
    tile = 256

    def kernel(x_ref, w_ref, gain_ref, normed_ref, values_ref, values_t_ref, acts_ref, acts_t_ref, slope_ref):
        normed = normalize(x_ref[...].astype(F32), gain_ref[0:1, :])
        normed_ref[...] = normed
        both = nn(normed, w_ref[...])
        acts, slope = gelu(both[:, width:])
        values = both[:, :width]
        values_ref[...] = values.astype(BF16)
        values_t_ref[...] = values.T.astype(BF16)
        acts_ref[...] = acts.astype(BF16)
        acts_t_ref[...] = acts.T.astype(BF16)
        slope_ref[...] = slope.astype(BF16)

    rows = lambda i: (i, 0)
    columns = lambda i: (0, i)
    return pl.pallas_call(
        kernel,
        grid=(total // tile,),
        in_specs=[
            pl.BlockSpec((tile, model), rows),
            pl.BlockSpec(weights.shape, lambda i: (0, 0)),
            pl.BlockSpec(gain.shape, lambda i: (0, 0)),
        ],
        out_specs=[
            pl.BlockSpec((tile, model), rows),
            pl.BlockSpec((tile, width), rows),
            pl.BlockSpec((width, tile), columns),
            pl.BlockSpec((tile, width), rows),
            pl.BlockSpec((width, tile), columns),
            pl.BlockSpec((tile, width), rows),
        ],
        out_shape=[
            jax.ShapeDtypeStruct((total, model), BF16),
            jax.ShapeDtypeStruct((total, width), BF16),
            jax.ShapeDtypeStruct((width, total), BF16),
            jax.ShapeDtypeStruct((total, width), BF16),
            jax.ShapeDtypeStruct((width, total), BF16),
            jax.ShapeDtypeStruct((total, width), BF16),
        ],
        compiler_params=pltpu.CompilerParams(vmem_limit_bytes=VMEM),
        cost_estimate=pl.CostEstimate(flops=2 * total * model * 2 * width, bytes_accessed=6 * total * model, transcendentals=0),
        name="begin",
    )(inputs, weights, gain)


def by_rows(mixed):
    if len(mixed.shape) == 2:
        return mixed.T
    return jnp.concatenate([mixed[c].T for c in range(mixed.shape[0])], axis=0)


def ends(x, mixed, flat, weights, width, gain, row, more):
    share, model = x.shape
    groups = weights.shape[0]
    hidden = (weights.shape[2] - 2 * width) // 2

    def kernel(*refs):
        x_ref, mixed_ref, gain_ref, up_ref, down_ref, side_ref = refs[:6]
        refs = refs[6:]
        middle_ref, normed_ref, hidden_ref, slope_ref, y_ref = refs[:5]
        acc = refs[-1]
        group = pl.program_id(0)

        @pl.when(group == 0)
        def _():
            total = x_ref[...].astype(F32)
            for j in range(groups):
                block = mixed_ref[j] if flat else by_rows(mixed_ref[j])
                total += nt(block, side_ref[j, :, 0:width])
            middle_ref[...] = total
            normed_ref[...] = normalize(total, gain_ref[row : row + 1, :])
            acc[...] = total

        normed = normed_ref[...]
        part = 256 if hidden % 256 == 0 else hidden
        ahead = nn(normed, up_ref[0, :, 0:part])
        for spot in range(0, hidden, part):
            pre = ahead
            if spot + part < hidden:
                ahead = nn(normed, up_ref[0, :, spot + part : spot + 2 * part])
            value, slope = gelu(pre)
            hidden_ref[0, :, spot : spot + part] = value.astype(BF16)
            slope_ref[0, :, spot : spot + part] = slope.astype(BF16)
        acc[...] += nt(hidden_ref[0], down_ref[0])

        @pl.when(group == groups - 1)
        def _():
            y = acc[...]
            y_ref[...] = y.astype(y_ref.dtype)
            if more:
                normed = normalize(y, gain_ref[row + 1 : row + 2, :])
                refs[5][...] = normed
                for j in range(groups):
                    refs[6][j] = nn(normed, side_ref[j, :, width : 2 * width]).T.astype(BF16)

    whole2, whole3 = (lambda g: (0, 0)), (lambda g: (0, 0, 0))
    in_specs = [
        pl.BlockSpec(x.shape, whole2),
        pl.BlockSpec(mixed.shape, lambda g: (0,) * mixed.ndim),
        pl.BlockSpec(gain.shape, whole2),
        pl.BlockSpec((1, model, hidden), lambda g: (g, 0, 0)),
        pl.BlockSpec((1, model, hidden), lambda g: (g, 0, 1)),
        pl.BlockSpec((groups, model, 2 * width), lambda g: (0, 0, hidden // width)),
    ]
    out_specs = [
        pl.BlockSpec((share, model), whole2),
        pl.BlockSpec((share, model), whole2),
        pl.BlockSpec((1, share, hidden), lambda g: (g, 0, 0)),
        pl.BlockSpec((1, share, hidden), lambda g: (g, 0, 0)),
        pl.BlockSpec((share, model), whole2),
    ]
    out_shape = [
        jax.ShapeDtypeStruct((share, model), F32),
        jax.ShapeDtypeStruct((share, model), BF16),
        jax.ShapeDtypeStruct((groups, share, hidden), BF16),
        jax.ShapeDtypeStruct((groups, share, hidden), BF16),
        jax.ShapeDtypeStruct((share, model), F32 if more else BF16),
    ]
    if more:
        out_specs += [pl.BlockSpec((share, model), whole2), pl.BlockSpec((groups, width, share), whole3)]
        out_shape += [
            jax.ShapeDtypeStruct((share, model), BF16),
            jax.ShapeDtypeStruct((groups, width, share), BF16),
        ]
    return pl.pallas_call(
        kernel,
        grid=(groups,),
        in_specs=in_specs,
        out_specs=out_specs,
        out_shape=out_shape,
        scratch_shapes=[pltpu.VMEM((share, model), F32)],
        compiler_params=pltpu.CompilerParams(vmem_limit_bytes=VMEM),
        cost_estimate=pl.CostEstimate(flops=4 * share * model * groups * hidden, bytes_accessed=4 * groups * model * hidden, transcendentals=0),
        name="ends",
    )(x, mixed, gain, weights, weights, weights)


def ends_back(grad, mixed, flat, weights, width, gain, row, record, after=None):
    middle, normed, hid, slope = record
    share, model = middle.shape
    groups = weights.shape[0]
    hidden = hid.shape[2]
    more = after is not None
    columns = 2 * hidden + (2 if more else 1) * width

    def kernel(*refs):
        grad_ref, mixed_ref, gain_ref, up_ref, down_ref, side_ref, middle_ref, normed_ref, hidden_ref, slope_ref = refs[:10]
        refs = refs[10:]
        if more:
            next_ref, next_normed_ref, dvalues_ref = refs[:3]
            refs = refs[3:]
        out_ref, dmiddle_ref, dmixed_ref, dgain_ref, total, low, low_t, normed_t, dnormed, grads_ref, side_grads, sems = refs
        group = pl.program_id(0)

        def leave(g):
            return pltpu.make_async_copy(grads_ref.at[g], out_ref.at[g, :, pl.ds(0, 2 * hidden)], sems.at[g])

        side_leave = pltpu.make_async_copy(
            side_grads, out_ref.at[:, :, pl.ds(2 * hidden, columns - 2 * hidden)], sems.at[groups]
        )

        @pl.when(group == 0)
        def _():
            g = grad_ref[...].astype(F32)
            dgain_ref[...] = jnp.zeros_like(dgain_ref)
            if more:
                pull = jnp.zeros((share, model), F32)
                next_t = next_normed_ref[...].T
                for j in range(groups):
                    dvalues = dvalues_ref[j].T
                    side_grads[j, :, width : 2 * width] = nn(next_t, dvalues).astype(BF16)
                    pull += nt(dvalues, side_ref[j, :, width : 2 * width])
                dx, dg = normalize_back(next_ref[...], gain_ref[row + 1 : row + 2, :], pull)
                g += dx
                dgain_ref[1:2, :] = dg
            total[...] = g
            low[...] = g.astype(BF16)
            low_t[...] = g.astype(BF16).T
            normed_t[...] = normed_ref[...].T
            dnormed[...] = jnp.zeros_like(dnormed)

        dpre = (slope_ref[0].astype(F32) * nn(low[...], down_ref[0])).astype(BF16)
        grads_ref[group, :, 0:hidden] = nn(normed_t[...], dpre).astype(BF16)
        grads_ref[group, :, hidden : 2 * hidden] = nn(low_t[...], hidden_ref[0]).astype(BF16)
        leave(group).start()
        dnormed[...] += nt(dpre, up_ref[0])

        @pl.when(group == groups - 1)
        def _():
            dx, dg = normalize_back(middle_ref[...], gain_ref[row : row + 1, :], dnormed[...])
            dmiddle = total[...] + dx
            dgain_ref[0:1, :] = dg
            dmiddle_ref[...] = dmiddle
            down = dmiddle.astype(BF16)
            down_t = down.T
            for j in range(groups):
                block = mixed_ref[j] if flat else by_rows(mixed_ref[j])
                side_grads[j, :, 0:width] = nn(down_t, block).astype(BF16)
                dmixed = nn(down, side_ref[j, :, 0:width])
                if flat:
                    dmixed_ref[j] = dmixed.astype(BF16)
                elif len(mixed.shape) == 3:
                    dmixed_ref[j] = dmixed.T.astype(BF16)
                else:
                    rows = mixed.shape[3]
                    for c in range(mixed.shape[1]):
                        dmixed_ref[j, c] = dmixed[c * rows : (c + 1) * rows].T.astype(BF16)
            side_leave.start()
            side_leave.wait()
            for g in range(groups):
                leave(g).wait()

    whole2, whole3 = (lambda g: (0, 0)), (lambda g: (0, 0, 0))
    whole = lambda a: pl.BlockSpec(a.shape, lambda g: (0,) * a.ndim)
    in_specs = [
        whole(grad),
        whole(mixed),
        whole(gain),
        pl.BlockSpec((1, model, hidden), lambda g: (g, 0, 0)),
        pl.BlockSpec((1, model, hidden), lambda g: (g, 0, 1)),
        pl.BlockSpec((groups, model, 2 * width), lambda g: (0, 0, hidden // width)),
        whole(middle),
        whole(normed),
        pl.BlockSpec((1, share, hidden), lambda g: (g, 0, 0)),
        pl.BlockSpec((1, share, hidden), lambda g: (g, 0, 0)),
    ]
    operands = [grad, mixed, gain, weights, weights, weights, middle, normed, hid, slope]
    if more:
        in_specs += [whole(a) for a in after]
        operands += list(after)
    out_specs = [
        ANY,
        pl.BlockSpec((share, model), whole2),
        whole(mixed),
        pl.BlockSpec((8, model), whole2),
    ]
    out_shape = [
        jax.ShapeDtypeStruct((groups, model, columns), BF16),
        jax.ShapeDtypeStruct((share, model), F32),
        jax.ShapeDtypeStruct(mixed.shape, BF16),
        jax.ShapeDtypeStruct((8, model), F32),
    ]
    scratch = [
        pltpu.VMEM((share, model), F32),
        pltpu.VMEM((share, model), BF16),
        pltpu.VMEM((model, share), BF16),
        pltpu.VMEM((model, share), BF16),
        pltpu.VMEM((share, model), F32),
        pltpu.VMEM((groups, model, 2 * hidden), BF16),
        pltpu.VMEM((groups, model, columns - 2 * hidden), BF16),
        DMA((groups + 1,)),
    ]
    return pl.pallas_call(
        kernel,
        grid=(groups,),
        in_specs=in_specs,
        out_specs=out_specs,
        out_shape=out_shape,
        scratch_shapes=scratch,
        compiler_params=pltpu.CompilerParams(vmem_limit_bytes=VMEM),
        cost_estimate=pl.CostEstimate(flops=8 * share * model * groups * hidden, bytes_accessed=8 * groups * model * hidden, transcendentals=0),
        name="ends_back",
    )(*operands)


def finish(back, weights, first, x, gain, dmiddle, gains, n, n_mp):
    groups, share, both = back.shape
    model, width = first.shape[1:]
    spot = weights.shape[2] // (2 * width) - 1
    pairs = n_mp // 2
    chunks = 4
    tall = share // chunks

    def kernel(back_ref, side_ref, first_ref, x_ref, gain_ref, dmiddle_ref, gains_ref, all_ref, sum_ref, out, here, one,
               two, far_send, far_recv, near_send, near_recv, on_send, on_recv, own_sem, g_send, g_recv, h_send, h_recv):
        me, place = lax.axis_index("mp"), lax.axis_index("dp")
        pair, core = me // 2, lax.rem(me, 2)
        twin = pair * 2 + 1 - core
        greet([("dp", n), ("mp", n_mp)])

        def rows(c):
            return pl.ds(c * tall, tall)

        def far(step, c):
            to = lax.rem(pair + step, pairs) * 2 + core
            return remote(
                out.at[rows(c)], all_ref.at[me, rows(c)], far_send.at[step, c], far_recv.at[step, c], "mp", to
            )

        def near(c):
            return remote(out.at[rows(c)], all_ref.at[me, rows(c)], near_send.at[c], near_recv.at[c], "mp", twin)

        def onward(step, c):
            source = lax.rem(pair + pairs - step, pairs) * 2 + core
            block = all_ref.at[source, rows(c)]
            return remote(block, block, on_send.at[step, c], on_recv.at[step, c], "mp", twin)

        total = jnp.zeros((1, model), F32)
        for c in range(chunks):
            span = slice(c * tall, (c + 1) * tall)
            pull = jnp.zeros((tall, model), F32)
            for j in range(groups):
                pull += nt(back_ref[j, span, 0:width], side_ref[j, :, width : 2 * width])
                pull += nt(back_ref[j, span, width:both], first_ref[j])
            dx, dg = normalize_back(x_ref[span, :].astype(F32), gain_ref[0:1, :], pull)
            out[span, :] = (dmiddle_ref[span, :] + dx).astype(BF16)
            total += dg
            for step in range(1, pairs):
                far(step, c).start()
            near(c).start()
        own = pltpu.make_async_copy(out, all_ref.at[me], own_sem)
        own.start()
        here[...] = gains_ref[...]
        here[0:1, :] = total
        one[me] = here[...]
        firsts = []
        for step in range(1, n_mp):
            to = lax.rem(me + step, n_mp)
            firsts.append(remote(here, one.at[me], g_send.at[step], g_recv.at[step], "mp", to))
            firsts[-1].start()
        for copy in firsts:
            copy.wait()
        total = one[0]
        for j in range(1, n_mp):
            total += one[j]
        two[place] = total

        def spread(step, there):
            return remote(two.at[place], two.at[there], h_send.at[step], h_recv.at[step], "dp", lax.rem(place + step, n))

        @pl.loop(1, n)
        def _(step):
            spread(step, place).start()

        for c in range(chunks):
            for step in range(1, pairs):
                far(step, c).wait_recv()
                onward(step, c).start()

        @pl.loop(1, n)
        def _(step):
            spread(step, place).wait_send()
            spread(step, lax.rem(place + n - step, n)).wait_recv()

        total = two[0]
        for j in range(1, n):
            total += two[j]
        sum_ref[...] = total
        for c in range(chunks):
            near(c).wait()
            for step in range(1, pairs):
                far(step, c).wait_send()
                onward(step, c).wait()
        own.wait()

    return pl.pallas_call(
        kernel,
        grid=(1,),
        in_specs=[
            pl.BlockSpec(back.shape, lambda i: (0, 0, 0)),
            pl.BlockSpec((groups, model, 2 * width), lambda i: (0, 0, spot)),
            pl.BlockSpec(first.shape, lambda i: (0, 0, 0)),
            pl.BlockSpec(x.shape, lambda i: (0, 0)),
            pl.BlockSpec(gain.shape, lambda i: (0, 0)),
            pl.BlockSpec(dmiddle.shape, lambda i: (0, 0)),
            pl.BlockSpec(gains.shape, lambda i: (0, 0)),
        ],
        out_specs=[ANY, pl.BlockSpec(gains.shape, lambda i: (0, 0))],
        out_shape=[
            jax.ShapeDtypeStruct((n_mp, share, model), BF16),
            jax.ShapeDtypeStruct(gains.shape, F32),
        ],
        scratch_shapes=[
            pltpu.VMEM((share, model), BF16),
            pltpu.VMEM(gains.shape, F32),
            pltpu.VMEM((n_mp,) + gains.shape, F32),
            pltpu.VMEM((n,) + gains.shape, F32),
            DMA((pairs, chunks)),
            DMA((pairs, chunks)),
            DMA((chunks,)),
            DMA((chunks,)),
            DMA((pairs, chunks)),
            DMA((pairs, chunks)),
            DMA,
            DMA((n_mp,)),
            DMA((n_mp,)),
            DMA((n,)),
            DMA((n,)),
        ],
        compiler_params=comm_params(4),
        name="finish",
    )(back, weights, first, x, gain, dmiddle, gains)


def per_device(
    n_dp,
    n_mp,
    tokens,
    lengths,
    norm_gain,
    w_value,
    w_out,
    w_up,
    w_down,
    synth_first,
    synth_second,
    random_table,
    cotangent,
):
    both = ("mp", "dp")
    place, rank = lax.axis_index("dp"), lax.axis_index("mp")
    total, model = tokens.shape
    share = total // n_mp
    size = total - MOST
    depth, width = w_value.shape[1], w_value.shape[2]
    hidden = w_up.shape[2]
    heads, rows, columns = random_table.shape
    near = rows == size and share % rows == 0 and n_dp in (2, 4, 6, 8)

    item_lengths = lengths[0]
    longest = jnp.argmax(item_lengths)
    start = (jnp.cumsum(item_lengths) - item_lengths)[longest]
    first = item_lengths[(longest + 1) % item_lengths.shape[0]].astype(jnp.int32).reshape(1, 1)

    gains = jnp.pad(norm_gain.reshape(4, depth).T, ((0, 0), (0, 124)))
    pack = jnp.concatenate([w_value[0], synth_first, gains], axis=1)
    table = synth_second.reshape(width, -1)
    corner = random_table[:, :, :size]
    if near:
        pack, table, corner = gather_weights([pack, table], corner.reshape(n_dp, -1, size), n_dp)
    else:
        begins = jnp.minimum(place * rows, size - rows)
        inside = (place * rows < size).astype(BF16)
        corner = lax.dynamic_update_slice(jnp.zeros((heads, size, size), BF16), corner * inside, (0, begins, 0))
        corner = lax.psum(corner, "dp")
        pack, table = lax.all_gather(pack, "dp"), lax.all_gather(table, "dp")
        table = table.transpose(1, 0, 2).reshape(width, total // size, size).transpose(1, 0, 2)
    pack = pack.reshape(model, -1)
    gain = jnp.pad(pack[:, 2 * width : 2 * width + 4].T.astype(F32), ((0, 4), (0, 0)))

    def whole(parts):
        joined = lax.all_gather(jnp.concatenate(parts, axis=1), both)
        return joined.reshape(n_mp, model, -1)

    weights_one = whole([w_up[0], w_down[0].T, w_out[0].T, w_value[1]])
    weights_two = [w_up[1], w_down[1].T, w_out[1].T, w_value[0]]

    inputs = turn(tokens, start, total)
    normed_one, values, values_t, acts, acts_t, slope = begin(inputs, pack[:, : 2 * width], gain)
    if near:
        mixed_one, lse, corner = dense_forward(first, acts, values, table, corner, n_dp, n_mp)
        corner = corner.reshape(heads, size, size)
    else:
        mixed, lse = dense_forward(first, acts, values, table)
        mixed_one = swap(mixed.reshape(n_mp, share, width), n_mp, 5)
    inputs = lax.dynamic_slice_in_dim(inputs, rank * share, share)
    *record_one, between, normed_two, parts = ends(
        inputs, mixed_one, True, weights_one, width, gain, 1, True
    )

    if near:
        values_all, mixed_two, short_t, table_lse, weights_two = table_forward(
            first, random_table, corner, parts, jnp.concatenate(weights_two, axis=1), n_dp, n_mp
        )
        weights_two = weights_two.reshape(n_mp, model, -1)
    else:
        weights_two = whole(weights_two)
        values_two = swap(parts, n_mp, 6, lanes_out=True)
        short_t = values_two[:, MOST:]
        values_all = lax.all_gather(values_two[:, :MOST], "dp")
        mixed, table_lse = random_forward(random_table, values_all)
        mixed = lax.all_to_all(mixed, "dp", 0, 0, tiled=True).transpose(1, 0, 2).reshape(width, total)
        mixed = jnp.concatenate([mixed[:, :MOST], short_forward(first, corner, short_t)], axis=1)
        mixed_two = swap(mixed, n_mp, 7, lanes_in=True)
    *record_two, result = ends(between, mixed_two, False, weights_two, width, gain, 3, False)
    early_first, _ = lax.optimization_barrier((synth_first, mixed_two))
    first_all = whole([early_first])

    grad = turn(cotangent, lax.rem(start + rank * share, total), share)
    grads_two, dmiddle, parts, dgain_two = ends_back(
        grad, mixed_two, False, weights_two, width, gain, 3, record_two
    )

    def scattered(grads, axes):
        grads = grads.reshape(-1, depth, grads.shape[-1])
        return lax.psum_scatter(grads, axes, scatter_dimension=0).astype(F32)

    if near:
        rows_upstream, dvalues, dcorner, grads_two = table_backward(
            first, random_table, corner, table_lse, short_t, parts, grads_two, n_dp, n_mp
        )
    else:
        upstream = swap(parts, n_mp, 8, lanes_out=True)
        dcorner, dshort = short_backward(first, corner, short_t, upstream[:, MOST:])
        dcorner = lax.dynamic_slice_in_dim(lax.psum(dcorner, "dp"), begins, rows, axis=1) * inside
        upstream = upstream.reshape(width, n_dp, rows).transpose(1, 0, 2)
        upstream = lax.all_to_all(upstream, "dp", 0, 0, tiled=True)
        valid = (place * rows < MOST).astype(F32).reshape(1, 1)
        dtable, dvalues = random_backward(valid, random_table, table_lse, values_all, upstream)
        dvalues = lax.psum_scatter(dvalues, "dp", scatter_dimension=0)
        dvalues = swap(jnp.concatenate([dvalues, dshort], axis=1), n_mp, 9, lanes_in=True)
        result = lax.all_gather(result, "mp")
        grads_two = scattered(grads_two, both)

    grads_one, dmiddle, parts, dgain_one = ends_back(
        dmiddle, mixed_one, True, weights_one, width, gain, 1, record_one, (between, normed_two, dvalues)
    )
    grads_one = scattered(grads_one, both)
    upstream = swap(parts, n_mp, 10).reshape(total, width)
    back_one = partial(dense_backward, first, acts, acts_t, values_t, upstream, table, lse, slope, normed_one)
    if near:
        back, entry_grad, second_grad, grads_two, result = back_one(
            grads_two.reshape(n_dp, depth, -1), result, n_dp, n_mp
        )
    else:
        back, entry_grad, second_grad = back_one()
    result = turn(result.reshape(total, model), total - start, total)
    back = back.reshape(n_mp, share, 2 * width)
    entry_grad = entry_grad.reshape(n_dp, depth, 2 * width)
    if near:
        back, entry_grad, second_grad, dcorner = last_exchange(
            back, [entry_grad, second_grad, dcorner.reshape(n_dp, -1, size)], n_dp, n_mp
        )
        dcorner = dcorner.reshape(heads, size, size)
    else:
        back = swap(back, n_mp, 11)
        entry_grad = lax.psum_scatter(entry_grad, "dp", scatter_dimension=0).astype(F32)
        second_grad = second_grad.transpose(1, 0, 2).reshape(width, n_dp, -1).transpose(1, 0, 2)
        second_grad = lax.psum_scatter(second_grad, "dp", scatter_dimension=0).astype(F32)
    gain_grad = jnp.concatenate([dgain_one[:1], dgain_one[:2], dgain_two[:1], jnp.zeros((4, model), F32)])
    input_grad, gain_grad = finish(back, weights_two, first_all, inputs, gain, dmiddle, gain_grad, n_dp, n_mp)
    input_grad = turn(input_grad.reshape(total, model), total - start, total)
    if near:
        upstream_last, _ = lax.optimization_barrier((rows_upstream, gain_grad))
        dtable = table_grad(random_table, table_lse, values_all, upstream_last, dcorner)
    else:
        dtable = dtable.at[:, :, :size].add(dcorner.astype(F32))

    gain_grad = lax.dynamic_slice_in_dim(gain_grad[:4], place * depth, depth, axis=1)
    out_at = slice(2 * hidden, 2 * hidden + width)
    return (
        result,
        input_grad,
        gain_grad.reshape(2, 2, depth),
        jnp.stack([entry_grad[:, :width], grads_one[:, 2 * hidden + width :]]),
        jnp.stack([grads_one[:, out_at].T, grads_two[:, out_at].T]),
        jnp.stack([grads_one[:, :hidden], grads_two[:, :hidden]]),
        jnp.stack([grads_one[:, hidden : 2 * hidden].T, grads_two[:, hidden : 2 * hidden].T]),
        entry_grad[:, width:],
        second_grad.reshape(heads, HD, -1),
        dtable,
    )


def solution(mesh):
    in_specs = (
        P("dp", None),
        P("dp", None),
        P(None, None, "dp"),
        P(None, "dp", "mp"),
        P(None, "mp", "dp"),
        P(None, "dp", "mp"),
        P(None, "mp", "dp"),
        P("dp", "mp"),
        P("mp", None, "dp"),
        P("mp", "dp", None),
        P("dp", None),
    )
    out_specs = (
        P("dp", None),
        P("dp", None),
        P(None, None, "dp"),
        P(None, "dp", "mp"),
        P(None, "mp", "dp"),
        P(None, "dp", "mp"),
        P(None, "mp", "dp"),
        P("dp", "mp"),
        P("mp", None, "dp"),
        P("mp", "dp", None),
    )
    return jax.shard_map(
        partial(per_device, mesh.shape["dp"], mesh.shape["mp"]),
        mesh=mesh,
        in_specs=in_specs,
        out_specs=out_specs,
        check_vma=False,
    )
```

profile of v0, /device:TPU:10, one launch (start us, length us, event | category | flops | bytes accessed | tf_op | source)
XLA Modules:
  0.0 617.8 jit_solution(9585997152366124697)
XLA Ops:
  9.1 1.0 slice_bitcast_fusion.5
  11.9 1.3 bitcast_reduce_fusion
  16.0 1.8 slice.74
  18.5 31.1 %gather_weights.1 = (bf16[8,96,512]{2,1,0:T(8,128)(2,1)}, bf16[8,192,256]{2,1,0:T(8,128)(2,1)}, bf16[96,256]{1,0:T(8,128)(2,1)}) custom-call(bf16[96,512]{1,0:T(8,128)(2,1)} %fusion.1.refs_0_, bf16[192,256]{1,0:T(8,128)(2,1)} %bitcast.110, bf16[8,96,256]{2,1,0:T(8,128)(2,1)} %bitcast.98), custom_call_target="tpu_custom_call" | custom-call | tf_op jit(solution)/shard_map/gather_weights/pallas_call | solution.py:425
  50.5 1.9 slice.97.w_ref
  54.7 5.5 turn.4.x_ref
  61.7 9.8 %begin.1 = (bf16[2048,768]{1,0:T(8,128)(2,1)}, bf16[2048,192]{1,0:T(8,128)(2,1)}, bf16[192,2048]{1,0:T(8,128)(2,1)}, bf16[2048,192]{1,0:T(8,128)(2,1)}, bf16[192...) custom-call(bf16[2048,768]{1,0:T(8,128)(2,1)} %turn.4.x_ref, bf16[768,384]{1,0:T(8,128)(2,1)} %slice.97.w_ref, ...), custom_call_target="tpu_custom_call" | custom-call | flops 1207959552 | bytes 9437184 | tf_op jit(solution)/shard_map/begin/pallas_call | solution.py:1529
  71.5 2.1 constant_dynamic-slice_fusion.1.refs_0_.x_ref
  73.6 41.9 %dense_forward.1 = (bf16[4,512,192]{2,1,0:T(8,128)(2,1)}, f32[2048,128]{1,0:T(8,128)}, bf16[8,96,256]{2,1,0:T(8,128)(2,1)}) custom-call(s32[1,1]{1,0:T(1,128)} %constant_dynamic-slice_fusion.2.first_ref, bf16[2048,192]{1,0:T(8,128)(2,1)} %get-tuple-element.67.acts_ref, bf16[2048,192]{1,0:T(8,128)(2,1)} %get-tuple-element.70.values_ref, ...), custom_call_target="tpu_custom_call" | custom-call | flops 9663676416 | bytes 3145728 | tf_op jit(solution)/shard_map/dense_forward/pallas_call | solution.py:1115
  115.5 16.8 %ends.2 = (f32[512,768]{1,0:T(8,128)}, bf16[512,768]{1,0:T(8,128)(2,1)}, bf16[4,512,768]{2,1,0:T(8,128)(2,1)}, bf16[4,512,768]{2,1,0:T(8,128)(2,1)}, f32[512,768...) custom-call(bf16[512,768]{1,0:T(8,128)(2,1)} %constant_dynamic-slice_fusion.1.refs_0_.x_ref, ...), custom_call_target="tpu_custom_call" | custom-call | flops 4831838208 | bytes 9437184 | tf_op jit(solution)/shard_map/ends/pallas_call | solution.py:1638
  132.3 109.8 %table_forward.1 = (bf16[8,192,1792]{2,1,0:T(8,128)(2,1)}, bf16[4,2,192,256]{3,2,1,0:T(8,128)(2,1)}, bf16[192,256]{1,0:T(8,128)(2,1)}, f32[3,256,128]{2,1,0:T(8,128)}, bf16[4,8,96,1920]{3,2,1,0:T(8,128)(2,1)}) custom-call(s32[1,1]{1,0:T(1,128)} %constant_dynamic-slice_fusion.2.first_ref, bf16[3,256,2048]{2,1,0:T(8,128)(2,1)} %table_ref.5, ...), custom_call_target="tpu_custom_call" | custom-call | tf_op jit(solution)/shard_map/table_forward/pallas_call | solution.py:642
  242.9 3.4 turn.5.refs_0_
  246.3 15.1 %ends.3 = (f32[512,768]{1,0:T(8,128)}, bf16[512,768]{1,0:T(8,128)(2,1)}, bf16[4,512,768]{2,1,0:T(8,128)(2,1)}, bf16[4,512,768]{2,1,0:T(8,128)(2,1)}, bf16[512,768]{1,0:T(8,128)(2,1)}) custom-call(f32[512,768]{1,0:T(8,128)} %get-tuple-element.78.refs_0_.refs_10_, bf16[4,2,192,256]{3,2,1,0:T(8,128)(2,1)} %get-tuple-element.76.refs_1_, ...), custom_call_target="tpu_custom_call" | custom-call | flops 4831838208 | bytes 9437184 | tf_op jit(solution)/shard_map/ends/pallas_call | solution.py:1638
  261.5 20.8 %ends_back.2 = (bf16[4,768,1728]{2,1,0:T(8,128)(2,1)}, f32[512,768]{1,0:T(8,128)}, bf16[4,2,192,256]{3,2,1,0:T(8,128)(2,1)}, f32[8,768]{1,0:T(8,128)}) custom-call(bf16[512,768]{1,0:T(8,128)(2,1)} %turn.5.refs_0_, bf16[4,2,192,256]{3,2,1,0:T(8,128)(2,1)} %get-tuple-element.76.refs_1_, f32[8,768]{1,0:T(8,128)} %pad_convert_fusion.gain_ref.refs_2_, ...), custom_call_target="tpu_custom_call" | custom-call | flops 9663676416 | bytes 18874368 | tf_op jit(solution)/shard_map/ends_back/pallas_call | solution.py:1766
  282.2 119.7 %table_backward.1 = (bf16[8,192,256]{2,1,0:T(8,128)(2,1)}, bf16[4,192,512]{2,1,0:T(8,128)(2,1)}, bf16[3,256,256]{2,1,0:T(8,128)(2,1)}, bf16[768,1728]{1,0:T(8,128)(2,1)}) custom-call(s32[1,1]{1,0:T(1,128)} %constant_dynamic-slice_fusion.2.first_ref, bf16[3,256,2048]{2,1,0:T(8,128)(2,1)} %table_ref.5, bf16[3,256,256]{2,1,0:T(8,128)(2,1)} %bitcast.100, ...), custom_call_target="tpu_custom_call" | custom-call | tf_op jit(solution)/shard_map/table_backward/pallas_call | solution.py:885
  402.0 24.6 %ends_back.3 = (bf16[4,768,1920]{2,1,0:T(8,128)(2,1)}, f32[512,768]{1,0:T(8,128)}, bf16[4,512,192]{2,1,0:T(8,128)(2,1)}, f32[8,768]{1,0:T(8,128)}) custom-call(f32[512,768]{1,0:T(8,128)} %get-tuple-element.83.refs_0_, bf16[4,512,192]{2,1,0:T(8,128)(2,1)} %get-tuple-element.74.refs_1_, f32[8,768]{1,0:T(8,128)} %pad_convert_fusion.gain_ref.refs_2_, ...), custom_call_target="tpu_custom_call" | custom-call | flops 9663676416 | bytes 18874368 | tf_op jit(solution)/shard_map/ends_back/pallas_call | solution.py:1766
  429.6 14.7 %swap.1 = bf16[4,512,192]{2,1,0:T(8,128)(2,1)} custom-call(bf16[4,512,192]{2,1,0:T(8,128)(2,1)} %get-tuple-element.94.x_ref), custom_call_target="tpu_custom_call" | custom-call | tf_op jit(solution)/shard_map/swap/pallas_call | solution.py:465
  444.3 52.4 %dense_backward.1 = (bf16[2048,384]{1,0:T(8,128)(2,1)}, bf16[768,384]{1,0:T(8,128)(2,1)}, bf16[8,192,256]{2,1,0:T(8,128)(2,1)}, f32[96,1728]{1,0:T(8,128)}, bf16[4,512,768]{2,1,0:T(8,128)(2,1)}) custom-call(s32[1,1]{1,0:T(1,128)} %constant_dynamic-slice_fusion.2.first_ref, bf16[2048,192]{1,0:T(8,128)(2,1)} %get-tuple-element.67.acts_ref, ...), custom_call_target="tpu_custom_call" | custom-call | flops 19327352832 | bytes 6291456 | tf_op jit(solution)/shard_map/dense_backward/pallas_call | solution.py:1251
  496.7 45.5 %last_exchange.1 = (bf16[4,512,384]{2,1,0:T(8,128)(2,1)}, f32[96,384]{1,0:T(8,128)}, f32[192,256]{1,0:T(8,128)}, bf16[8,96,256]{2,1,0:T(8,128)(2,1)}) custom-call(bf16[4,512,384]{2,1,0:T(8,128)(2,1)} %bitcast.97, bf16[8,96,384]{2,1,0:T(8,128)(2,1)} %bitcast.104, bf16[8,192,256]{2,1,0:T(8,128)(2,1)} %get-tuple-element.103.refs_2_, bf16[8,96,256]{2,1,0:T(8,128)(2,1)} %bitcast.105), custom_call_target="tpu_custom_call" | custom-call | tf_op jit(solution)/shard_map/last_exchange/pallas_call | solution.py:965
  542.2 4.9 turn.6
  548.7 42.3 %finish.1 = (bf16[4,512,768]{2,1,0:T(8,128)(2,1)}, f32[8,768]{1,0:T(8,128)}) custom-call(bf16[4,512,384]{2,1,0:T(8,128)(2,1)} %get-tuple-element.105.back_ref, bf16[4,768,1920]{2,1,0:T(8,128)(2,1)} %bitcast.86, bf16[4,768,192]{2,1,0:T(8,128)(2,1)} %bitcast.96, bf16[512,768]{1,0:T(8,128)(2,1)} %constant_dynamic-slice_fusion.1.refs_0_.x_ref, ...), custom_call_target="tpu_custom_call" | custom-call | tf_op jit(solution)/shard_map/finish/pallas_call | solution.py:1869
  591.7 4.9 turn.7
  596.6 8.6 %table_grad.1 = f32[3,256,2048]{2,1,0:T(8,128)} custom-call(bf16[3,256,2048]{2,1,0:T(8,128)(2,1)} %table_ref.5, f32[3,256,128]{2,1,0:T(8,128)} %get-tuple-element.89.lse_ref, bf16[8,192,1792]{2,1,0:T(8,128)(2,1)} %get-tuple-element.116.values_ref, bf16[8,192,256]{2,1,0:T(8,128)(2,1)} %get-tuple-element.118.up_ref, bf16[3,256,256]{2,1,0:T(8,128)(2,1)} %bitcast.106), custom_call_target="tpu_custom_call" | custom-call | tf_op jit(solution)/shard_map/table_grad/pallas_call | solution.py:1445
  605.8 1.1 bitcast_convert_fusion
  (53 shorter events, 18.5 us)
Async XLA Ops:
  7.2 45.3 %copy-start.4 = (s32[1,3]{1,0:T(1,128)S(1)}, s32[1,3]{1,0:T(1,128)}, u32[]{:S(2)}) copy-start(s32[1,3]{1,0:T(1,128)} %param.12) | copy-start | bytes 40
  7.2 10.6 %copy-start.2 = (bf16[96,192]{1,0:T(8,128)(2,1)S(1)}, bf16[96,192]{1,0:T(8,128)(2,1)}, u32[]{:S(2)}) copy-start(bf16[96,192]{1,0:T(8,128)(2,1)} %param.18) | copy-start | bytes 110596
  7.2 108.3 %all-gather.5.cloned.1.call-start = ((), (), s32[]{:S(2)}) async-start(), calls=%async_computation.2 | async-start | bytes 12165120 | tf_op jit(solution)/shard_map/all_gather | solution.py:1955
  11.9 536.8 %all-gather.7.cloned.1.call-start = ((), (), s32[]{:S(2)}) async-start(), calls=%async_computation.3 | async-start | bytes 1622016 | tf_op jit(solution)/shard_map/all_gather | solution.py:1955
  242.2 363.6 %reduce-scatter.2.cloned.1.call-start = ((), (), s32[]{:S(2)}) async-start(), calls=%async_computation.1 | async-start | bytes 12165120 | tf_op jit(solution)/shard_map/reduce_scatter | solution.py:1999
  542.2 5.6 copy-start.1
  542.2 6.4 %copy-start = (f32[96,1728]{1,0:T(8,128)S(1)}, f32[96,1728]{1,0:T(8,128)}, u32[]{:S(2)}) copy-start(f32[96,1728]{1,0:T(8,128)} %get-tuple-element.114) | copy-start | bytes 1990660
  605.8 4.5 copy-start.3
Sparse Core Ops, SparseCore 0:
  12.0 100.2 all-gather.4
  242.3 61.5 all-gather.6
  426.8 170.5 reduce-scatter.1
where the time goes:
time: 622 us; the launch traced here: 618 us
  Pallas kernels  572 us (92%)
  local copies, waits for them, and re-layouts  20.5 us (3%)
  between operations  18.2 us (3%)
  other arithmetic  7 us (1%)
    pallas_call x1, Pallas kernels, table_backward(): pl.pallas_call(kernel, in_specs=[SCALAR] + [INTO] * 5 + [ANY], out_specs=...  120 us
    pallas_call x1, Pallas kernels, table_forward(): pl.pallas_call(kernel, in_specs=[SCALAR, INTO, INTO, INTO, ANY], out_spec...  110 us
    pallas_call x1, Pallas kernels, dense_backward(): pl.pallas_call(kernel, grid=(tiles + 1,), in_specs=[pl.BlockSpec(memory_s...  52.4 us
    pallas_call x1, Pallas kernels, last_exchange(): pl.pallas_call(kernel, in_specs=[ANY] + [INTO] * count, out_specs=[ANY] +...  45.5 us
    pallas_call x2, Pallas kernels, ends_back(): pl.pallas_call(kernel, grid=(groups,), in_specs=in_specs, out_specs=out_s...  45.4 us
    pallas_call x1, Pallas kernels, finish(): pl.pallas_call(kernel, grid=(1,), in_specs=[pl.BlockSpec(back.shape, lamb...  42.3 us
    pallas_call x1, Pallas kernels, dense_forward(): pl.pallas_call(kernel, grid=(tiles + 1,), in_specs=[pl.BlockSpec(memory_s...  41.9 us
    pallas_call x2, Pallas kernels, ends(): pl.pallas_call(kernel, grid=(groups,), in_specs=in_specs, out_specs=out_s...  32 us
  transfers between devices with their start and end apart: 3, of which 0 were waited for; matrix products, arithmetic and copies ran while one was open for 3% of the time, Pallas kernels for 72%

commit v1 on v0

--- a/solution.py
+++ b/solution.py
@@ -1518,10 +1518,11 @@
         both = nn(normed, w_ref[...])
         acts, slope = gelu(both[:, width:])
         values = both[:, :width]
-        values_ref[...] = values.astype(BF16)
-        values_t_ref[...] = values.T.astype(BF16)
-        acts_ref[...] = acts.astype(BF16)
-        acts_t_ref[...] = acts.T.astype(BF16)
+        values, acts = values.astype(BF16), acts.astype(BF16)
+        values_ref[...] = values
+        values_t_ref[...] = values.T
+        acts_ref[...] = acts
+        acts_t_ref[...] = acts.T
         slope_ref[...] = slope.astype(BF16)
 
     rows = lambda i: (i, 0)

time: 622 us -> 620 us (level)
  no operation moved by 1% of the time
where the time goes in v1:
time: 620 us; the launch traced here: 616 us
  Pallas kernels  570 us (92%)
  local copies, waits for them, and re-layouts  20.5 us (3%)
  between operations  18.2 us (3%)
  other arithmetic  7 us (1%)
    pallas_call x1, Pallas kernels, table_backward(): pl.pallas_call(kernel, in_specs=[SCALAR] + [INTO] * 5 + [ANY], out_specs=...  119 us
    pallas_call x1, Pallas kernels, table_forward(): pl.pallas_call(kernel, in_specs=[SCALAR, INTO, INTO, INTO, ANY], out_spec...  111 us
    pallas_call x1, Pallas kernels, dense_backward(): pl.pallas_call(kernel, grid=(tiles + 1,), in_specs=[pl.BlockSpec(memory_s...  52 us
    pallas_call x1, Pallas kernels, last_exchange(): pl.pallas_call(kernel, in_specs=[ANY] + [INTO] * count, out_specs=[ANY] +...  45.7 us
    pallas_call x2, Pallas kernels, ends_back(): pl.pallas_call(kernel, grid=(groups,), in_specs=in_specs, out_specs=out_s...  45.4 us
    pallas_call x1, Pallas kernels, finish(): pl.pallas_call(kernel, grid=(1,), in_specs=[pl.BlockSpec(back.shape, lamb...  42.1 us
    pallas_call x1, Pallas kernels, dense_forward(): pl.pallas_call(kernel, grid=(tiles + 1,), in_specs=[pl.BlockSpec(memory_s...  41 us
    pallas_call x2, Pallas kernels, ends(): pl.pallas_call(kernel, grid=(groups,), in_specs=in_specs, out_specs=out_s...  32 us
  transfers between devices with their start and end apart: 3, of which 0 were waited for; matrix products, arithmetic and copies ran while one was open for 3% of the time, Pallas kernels for 72%

profile of v1, /device:TPU:10, one launch (start us, length us, event | category | flops | bytes accessed | tf_op | source)
XLA Modules:
  0.0 616.1 jit_solution(12956287707167459812)
XLA Ops:
  9.1 1.0 slice_bitcast_fusion.5
  11.9 1.3 bitcast_reduce_fusion
  16.0 1.8 slice.74
  18.5 31.1 %gather_weights.1 = (bf16[8,96,512]{2,1,0:T(8,128)(2,1)}, bf16[8,192,256]{2,1,0:T(8,128)(2,1)}, bf16[96,256]{1,0:T(8,128)(2,1)}) custom-call(bf16[96,512]{1,0:T(8,128)(2,1)} %fusion.1.refs_0_, bf16[192,256]{1,0:T(8,128)(2,1)} %bitcast.110, bf16[8,96,256]{2,1,0:T(8,128)(2,1)} %bitcast.98), custom_call_target="tpu_custom_call" | custom-call | tf_op jit(solution)/shard_map/gather_weights/pallas_call | solution.py:425
  50.5 1.9 slice.97.w_ref
  54.7 5.5 turn.4.x_ref
  61.7 9.8 %begin.1 = (bf16[2048,768]{1,0:T(8,128)(2,1)}, bf16[2048,192]{1,0:T(8,128)(2,1)}, bf16[192,2048]{1,0:T(8,128)(2,1)}, bf16[2048,192]{1,0:T(8,128)(2,1)}, bf16[192...) custom-call(bf16[2048,768]{1,0:T(8,128)(2,1)} %turn.4.x_ref, bf16[768,384]{1,0:T(8,128)(2,1)} %slice.97.w_ref, ...), custom_call_target="tpu_custom_call" | custom-call | flops 1207959552 | bytes 9437184 | tf_op jit(solution)/shard_map/begin/pallas_call | solution.py:1530
  71.4 2.1 constant_dynamic-slice_fusion.1.refs_0_.x_ref
  73.5 41.0 %dense_forward.1 = (bf16[4,512,192]{2,1,0:T(8,128)(2,1)}, f32[2048,128]{1,0:T(8,128)}, bf16[8,96,256]{2,1,0:T(8,128)(2,1)}) custom-call(s32[1,1]{1,0:T(1,128)} %constant_dynamic-slice_fusion.2.first_ref, bf16[2048,192]{1,0:T(8,128)(2,1)} %get-tuple-element.67.acts_ref, bf16[2048,192]{1,0:T(8,128)(2,1)} %get-tuple-element.70.values_ref, ...), custom_call_target="tpu_custom_call" | custom-call | flops 9663676416 | bytes 3145728 | tf_op jit(solution)/shard_map/dense_forward/pallas_call | solution.py:1115
  114.5 16.8 %ends.2 = (f32[512,768]{1,0:T(8,128)}, bf16[512,768]{1,0:T(8,128)(2,1)}, bf16[4,512,768]{2,1,0:T(8,128)(2,1)}, bf16[4,512,768]{2,1,0:T(8,128)(2,1)}, f32[512,768...) custom-call(bf16[512,768]{1,0:T(8,128)(2,1)} %constant_dynamic-slice_fusion.1.refs_0_.x_ref, ...), custom_call_target="tpu_custom_call" | custom-call | flops 4831838208 | bytes 9437184 | tf_op jit(solution)/shard_map/ends/pallas_call | solution.py:1639
  131.4 110.6 %table_forward.1 = (bf16[8,192,1792]{2,1,0:T(8,128)(2,1)}, bf16[4,2,192,256]{3,2,1,0:T(8,128)(2,1)}, bf16[192,256]{1,0:T(8,128)(2,1)}, f32[3,256,128]{2,1,0:T(8,128)}, bf16[4,8,96,1920]{3,2,1,0:T(8,128)(2,1)}) custom-call(s32[1,1]{1,0:T(1,128)} %constant_dynamic-slice_fusion.2.first_ref, bf16[3,256,2048]{2,1,0:T(8,128)(2,1)} %table_ref.5, ...), custom_call_target="tpu_custom_call" | custom-call | tf_op jit(solution)/shard_map/table_forward/pallas_call | solution.py:642
  242.7 3.4 turn.5.refs_0_
  246.1 15.1 %ends.3 = (f32[512,768]{1,0:T(8,128)}, bf16[512,768]{1,0:T(8,128)(2,1)}, bf16[4,512,768]{2,1,0:T(8,128)(2,1)}, bf16[4,512,768]{2,1,0:T(8,128)(2,1)}, bf16[512,768]{1,0:T(8,128)(2,1)}) custom-call(f32[512,768]{1,0:T(8,128)} %get-tuple-element.78.refs_0_.refs_10_, bf16[4,2,192,256]{3,2,1,0:T(8,128)(2,1)} %get-tuple-element.76.refs_1_, ...), custom_call_target="tpu_custom_call" | custom-call | flops 4831838208 | bytes 9437184 | tf_op jit(solution)/shard_map/ends/pallas_call | solution.py:1639
  261.2 20.8 %ends_back.2 = (bf16[4,768,1728]{2,1,0:T(8,128)(2,1)}, f32[512,768]{1,0:T(8,128)}, bf16[4,2,192,256]{3,2,1,0:T(8,128)(2,1)}, f32[8,768]{1,0:T(8,128)}) custom-call(bf16[512,768]{1,0:T(8,128)(2,1)} %turn.5.refs_0_, bf16[4,2,192,256]{3,2,1,0:T(8,128)(2,1)} %get-tuple-element.76.refs_1_, f32[8,768]{1,0:T(8,128)} %pad_convert_fusion.gain_ref.refs_2_, ...), custom_call_target="tpu_custom_call" | custom-call | flops 9663676416 | bytes 18874368 | tf_op jit(solution)/shard_map/ends_back/pallas_call | solution.py:1767
  282.0 118.7 %table_backward.1 = (bf16[8,192,256]{2,1,0:T(8,128)(2,1)}, bf16[4,192,512]{2,1,0:T(8,128)(2,1)}, bf16[3,256,256]{2,1,0:T(8,128)(2,1)}, bf16[768,1728]{1,0:T(8,128)(2,1)}) custom-call(s32[1,1]{1,0:T(1,128)} %constant_dynamic-slice_fusion.2.first_ref, bf16[3,256,2048]{2,1,0:T(8,128)(2,1)} %table_ref.5, bf16[3,256,256]{2,1,0:T(8,128)(2,1)} %bitcast.100, ...), custom_call_target="tpu_custom_call" | custom-call | tf_op jit(solution)/shard_map/table_backward/pallas_call | solution.py:885
  400.7 24.6 %ends_back.3 = (bf16[4,768,1920]{2,1,0:T(8,128)(2,1)}, f32[512,768]{1,0:T(8,128)}, bf16[4,512,192]{2,1,0:T(8,128)(2,1)}, f32[8,768]{1,0:T(8,128)}) custom-call(f32[512,768]{1,0:T(8,128)} %get-tuple-element.83.refs_0_, bf16[4,512,192]{2,1,0:T(8,128)(2,1)} %get-tuple-element.74.refs_1_, f32[8,768]{1,0:T(8,128)} %pad_convert_fusion.gain_ref.refs_2_, ...), custom_call_target="tpu_custom_call" | custom-call | flops 9663676416 | bytes 18874368 | tf_op jit(solution)/shard_map/ends_back/pallas_call | solution.py:1767
  428.3 14.8 %swap.1 = bf16[4,512,192]{2,1,0:T(8,128)(2,1)} custom-call(bf16[4,512,192]{2,1,0:T(8,128)(2,1)} %get-tuple-element.94.x_ref), custom_call_target="tpu_custom_call" | custom-call | tf_op jit(solution)/shard_map/swap/pallas_call | solution.py:465
  443.1 52.0 %dense_backward.1 = (bf16[2048,384]{1,0:T(8,128)(2,1)}, bf16[768,384]{1,0:T(8,128)(2,1)}, bf16[8,192,256]{2,1,0:T(8,128)(2,1)}, f32[96,1728]{1,0:T(8,128)}, bf16[4,512,768]{2,1,0:T(8,128)(2,1)}) custom-call(s32[1,1]{1,0:T(1,128)} %constant_dynamic-slice_fusion.2.first_ref, bf16[2048,192]{1,0:T(8,128)(2,1)} %get-tuple-element.67.acts_ref, ...), custom_call_target="tpu_custom_call" | custom-call | flops 19327352832 | bytes 6291456 | tf_op jit(solution)/shard_map/dense_backward/pallas_call | solution.py:1251
  495.1 45.7 %last_exchange.1 = (bf16[4,512,384]{2,1,0:T(8,128)(2,1)}, f32[96,384]{1,0:T(8,128)}, f32[192,256]{1,0:T(8,128)}, bf16[8,96,256]{2,1,0:T(8,128)(2,1)}) custom-call(bf16[4,512,384]{2,1,0:T(8,128)(2,1)} %bitcast.97, bf16[8,96,384]{2,1,0:T(8,128)(2,1)} %bitcast.104, bf16[8,192,256]{2,1,0:T(8,128)(2,1)} %get-tuple-element.103.refs_2_, bf16[8,96,256]{2,1,0:T(8,128)(2,1)} %bitcast.105), custom_call_target="tpu_custom_call" | custom-call | tf_op jit(solution)/shard_map/last_exchange/pallas_call | solution.py:965
  540.8 4.9 turn.6
  547.2 42.1 %finish.1 = (bf16[4,512,768]{2,1,0:T(8,128)(2,1)}, f32[8,768]{1,0:T(8,128)}) custom-call(bf16[4,512,384]{2,1,0:T(8,128)(2,1)} %get-tuple-element.105.back_ref, bf16[4,768,1920]{2,1,0:T(8,128)(2,1)} %bitcast.86, bf16[4,768,192]{2,1,0:T(8,128)(2,1)} %bitcast.96, bf16[512,768]{1,0:T(8,128)(2,1)} %constant_dynamic-slice_fusion.1.refs_0_.x_ref, ...), custom_call_target="tpu_custom_call" | custom-call | tf_op jit(solution)/shard_map/finish/pallas_call | solution.py:1870
  590.1 4.9 turn.7
  595.0 8.6 %table_grad.1 = f32[3,256,2048]{2,1,0:T(8,128)} custom-call(bf16[3,256,2048]{2,1,0:T(8,128)(2,1)} %table_ref.5, f32[3,256,128]{2,1,0:T(8,128)} %get-tuple-element.89.lse_ref, bf16[8,192,1792]{2,1,0:T(8,128)(2,1)} %get-tuple-element.116.values_ref, bf16[8,192,256]{2,1,0:T(8,128)(2,1)} %get-tuple-element.118.up_ref, bf16[3,256,256]{2,1,0:T(8,128)(2,1)} %bitcast.106), custom_call_target="tpu_custom_call" | custom-call | tf_op jit(solution)/shard_map/table_grad/pallas_call | solution.py:1445
  604.2 1.1 bitcast_convert_fusion
  (53 shorter events, 18.5 us)
Async XLA Ops:
  7.2 45.3 %copy-start.4 = (s32[1,3]{1,0:T(1,128)S(1)}, s32[1,3]{1,0:T(1,128)}, u32[]{:S(2)}) copy-start(s32[1,3]{1,0:T(1,128)} %param.12) | copy-start | bytes 40
  7.2 10.6 %copy-start.2 = (bf16[96,192]{1,0:T(8,128)(2,1)S(1)}, bf16[96,192]{1,0:T(8,128)(2,1)}, u32[]{:S(2)}) copy-start(bf16[96,192]{1,0:T(8,128)(2,1)} %param.18) | copy-start | bytes 110596
  7.2 107.3 %all-gather.5.cloned.1.call-start = ((), (), s32[]{:S(2)}) async-start(), calls=%async_computation.2 | async-start | bytes 12165120 | tf_op jit(solution)/shard_map/all_gather | solution.py:1956
  11.9 535.3 %all-gather.7.cloned.1.call-start = ((), (), s32[]{:S(2)}) async-start(), calls=%async_computation.3 | async-start | bytes 1622016 | tf_op jit(solution)/shard_map/all_gather | solution.py:1956
  242.0 362.2 %reduce-scatter.2.cloned.1.call-start = ((), (), s32[]{:S(2)}) async-start(), calls=%async_computation.1 | async-start | bytes 12165120 | tf_op jit(solution)/shard_map/reduce_scatter | solution.py:2000
  540.7 5.6 copy-start.1
  540.7 6.4 %copy-start = (f32[96,1728]{1,0:T(8,128)S(1)}, f32[96,1728]{1,0:T(8,128)}, u32[]{:S(2)}) copy-start(f32[96,1728]{1,0:T(8,128)} %get-tuple-element.114) | copy-start | bytes 1990660
  604.2 4.5 copy-start.3
Sparse Core Ops, SparseCore 0:
  12.0 100.2 all-gather.4
  242.1 59.6 all-gather.6
  425.5 168.7 reduce-scatter.1
